TPU v7x, 512 devices: a whole 4x4x16 slice. The times are simulated.
512 devices in a mesh: rep: 4 (over x_lo, core), ty: 8 (over x_hi, y), tx: 16 (over z).
Axes of the slice: x: 4 (x_hi: 2, x_lo: 2; x = x_hi * 2 + x_lo), y: 4, z: 16, core: 2. Of those that a mesh axis runs over, the one named last changes fastest.
Arguments:
- latent: bfloat16 [16, 16, 32, 3072], P('tx', 'ty', None, 'rep'), may hold values from -6 to 6
- in_weight: bfloat16 [3072, 1920], P(('rep', 'tx')), may hold values from -0.109375 to 0.109375
- qkv_weight: bfloat16 [1920, 3072], P('tx', 'rep'), may hold values from -2 to 2
- out_weight: bfloat16 [1024, 1920], P('rep', 'tx'), may hold values from -0.1875 to 0.1875
- norm_gain: bfloat16 [1920], replicated, may hold values from 0.099609375 to 1.8984375
- extents: int32 [8, 16, 4], P('ty', 'tx'), may hold values from 1 to 4, as said below
Outputs:
- block_out: bfloat16 [16, 64, 128, 1920], P('rep', 'ty', 'tx')
Inputs may be any that keep to these rules, and one draw needn't show every extreme that they name: `extents`: each entry is a reach in fine cells; some tile reaches 4 on every side and some tile reaches 1 on every side.
All inputs are finite; a program needn't handle non-finite values.
Results may differ from a plain program's by a relative error of at most 0.04.
Values may be sent and summed in bfloat16 or wider, within the bound.
No kernel may reach another device: no remote copies, remote signals or barrier semaphores. Data moves between devices by JAX's collectives and lax.ppermute only.
A program may use at most 128 MiB of HBM per device.

v0:
```python
import jax
import jax.numpy as jnp
from jax import lax
from jax.sharding import PartitionSpec as P

HD = 64
U = 4
FT = 4
R = 4


precise_mode = lax.Precision.HIGHEST


def padded(cells, sides, width):
    for axis, dim in sides:
        count = lax.axis_size(axis)
        ends = count - 1
        head = lax.slice_in_dim(cells, 0, width, axis=dim)
        tail = lax.slice_in_dim(cells, cells.shape[dim] - width, cells.shape[dim], axis=dim)
        cells = jnp.concatenate(
            [
                lax.ppermute(tail, axis, [(i, (i + 1) % count) for i in range(ends)]),
                cells,
                lax.ppermute(head, axis, [((i + 1) % count, i) for i in range(ends)]),
            ],
            axis=dim,
        )
    return cells


def interp_matrix(coarse_cells, factor):
    fine_index = jnp.arange(coarse_cells * factor, dtype=jnp.int32)
    coarse_index = fine_index // factor
    offsets = ((fine_index % factor).astype(jnp.float32) + 0.5) / factor - 0.5
    columns = jnp.arange(coarse_cells + 2, dtype=jnp.int32)
    centre = (columns[None, :] == coarse_index[:, None] + 1).astype(jnp.float32) * (
        1.0 - jnp.abs(offsets)
    )[:, None]
    before = (columns[None, :] == coarse_index[:, None]).astype(jnp.float32) * jnp.maximum(
        -offsets, 0.0
    )[:, None]
    following = (columns[None, :] == coarse_index[:, None] + 2).astype(jnp.float32) * jnp.maximum(
        offsets, 0.0
    )[:, None]
    return centre + before + following


def clamp_edges(field_data, at_first, at_last, axis_dim):
    length = field_data.shape[axis_dim]
    first_rim = jnp.where(
        at_first,
        lax.slice_in_dim(field_data, 1, 2, axis=axis_dim),
        lax.slice_in_dim(field_data, 0, 1, axis=axis_dim),
    )
    last_rim = jnp.where(
        at_last,
        lax.slice_in_dim(field_data, length - 2, length - 1, axis=axis_dim),
        lax.slice_in_dim(field_data, length - 1, length, axis=axis_dim),
    )
    middle = lax.slice_in_dim(field_data, 1, length - 1, axis=axis_dim)
    return jnp.concatenate([first_rim, middle, last_rim], axis=axis_dim)


def window_allowed(row_tile, col_tile, extent, tile_rows, tile_cols, grid_rows, grid_cols):
    local_rows = jnp.arange(tile_rows + 2 * R, dtype=jnp.int32)
    local_cols = jnp.arange(tile_cols + 2 * R, dtype=jnp.int32)
    global_rows = row_tile * tile_rows - R + local_rows
    global_cols = col_tile * tile_cols - R + local_cols
    row_valid = (
        (global_rows >= 0)
        & (global_rows < grid_rows)
        & (local_rows >= R - extent[0])
        & (local_rows < R + tile_rows + extent[1])
    )
    col_valid = (
        (global_cols >= 0)
        & (global_cols < grid_cols)
        & (local_cols >= R - extent[2])
        & (local_cols < R + tile_cols + extent[3])
    )
    return row_valid[:, None] & col_valid[None, :]


def window_attend(queries, keys_window, values_window, allowed):
    frame_total = queries.shape[0]
    head_depth = queries.shape[-1]
    groups = frame_total // FT
    flat_query = queries.reshape(groups, -1, head_depth)
    flat_key = keys_window.reshape(groups, -1, head_depth)
    flat_value = values_window.reshape(groups, -1, head_depth)
    scores = jnp.einsum(
        "gqd,gkd->gqk", flat_query, flat_key, preferred_element_type=jnp.float32
    ) * head_depth ** (-0.5)
    key_allowed = jnp.broadcast_to(allowed[None], (FT,) + allowed.shape).reshape(-1)
    scores = jnp.where(key_allowed[None, None, :], scores, -1e30)
    highest = jnp.max(scores, axis=-1, keepdims=True)
    weights = jnp.exp(scores - highest)
    probabilities = (weights / jnp.sum(weights, axis=-1, keepdims=True)).astype(jnp.bfloat16)
    mixture = jnp.einsum(
        "gqk,gkd->gqd", probabilities, flat_value, preferred_element_type=jnp.float32
    )
    return mixture.astype(jnp.bfloat16).reshape(queries.shape)


def row_adder(flat_rows, section):
    return jnp.dot(flat_rows, section, preferred_element_type=jnp.float32)


def body(latent, in_weight, qkv_weight, out_weight, norm_gain, extents):
    row_devices = lax.axis_size("ty")
    col_devices = lax.axis_size("tx")
    rep_devices = lax.axis_size("rep")
    row_place = lax.axis_index("ty")
    col_place = lax.axis_index("tx")
    rep_place = lax.axis_index("rep")
    coarse_tiles = lax.all_to_all(latent, "tx", split_axis=2, concat_axis=0, tiled=True)
    coarse_tiles = padded(coarse_tiles, (("ty", 1), ("tx", 2)), 1)
    frame_count, coarse_rows, coarse_cols, channels = coarse_tiles.shape
    flat_tiles = coarse_tiles.reshape(-1, channels)
    coarse = row_adder(flat_tiles, lax.all_gather(in_weight, "tx", axis=0, tiled=True))
    coarse = lax.psum(coarse, "rep").reshape(frame_count, coarse_rows, coarse_cols, -1)
    coarse = clamp_edges(coarse, row_place == 0, row_place == row_devices - 1, 1)
    coarse = clamp_edges(coarse, col_place == 0, col_place == col_devices - 1, 2)
    inner_rows = coarse.shape[1] - 2
    inner_cols = coarse.shape[2] - 2
    tile_rows = inner_rows * U
    tile_cols = inner_cols * U
    model_width = coarse.shape[3]
    row_matrix = interp_matrix(inner_rows, U)
    col_matrix = interp_matrix(inner_cols, U)
    tall_field = jnp.einsum("hp,fpqc->fhqc", row_matrix, coarse, precision=precise_mode)
    hidden = jnp.einsum("wq,fhqc->fhwc", col_matrix, tall_field, precision=precise_mode).astype(
        jnp.bfloat16
    )
    token_count = frame_count * tile_rows * tile_cols
    flat_hidden = hidden.reshape(token_count, model_width)
    widened = flat_hidden.astype(jnp.float32)
    scale_rows = lax.rsqrt(jnp.mean(widened * widened, axis=-1, keepdims=True) + 1e-06)
    flat_normed = (widened * scale_rows * norm_gain.astype(jnp.float32)).astype(jnp.bfloat16)
    project = row_adder(flat_normed, lax.all_gather(qkv_weight, "tx", axis=0, tiled=True))
    project = project.astype(jnp.bfloat16).reshape(frame_count, tile_rows, tile_cols, -1, 3, HD)
    group_heads = project.shape[3]
    queries = project[:, :, :, :, 0, :]
    key_part = project[:, :, :, :, 1, :].reshape(
        frame_count, tile_rows, tile_cols, group_heads * HD
    )
    value_part = project[:, :, :, :, 2, :].reshape(
        frame_count, tile_rows, tile_cols, group_heads * HD
    )
    key_value = jnp.stack([key_part, value_part], 0)
    key_value = padded(key_value, (("ty", 2), ("tx", 3)), R)
    window_keys = key_value[0].reshape(
        frame_count, tile_rows + 2 * R, tile_cols + 2 * R, group_heads, HD
    )
    window_values = key_value[1].reshape(
        frame_count, tile_rows + 2 * R, tile_cols + 2 * R, group_heads, HD
    )
    allowed = window_allowed(
        row_place,
        col_place,
        extents.reshape(4),
        tile_rows,
        tile_cols,
        row_devices * tile_rows,
        col_devices * tile_cols,
    )
    outputs = []
    for head_index in range(group_heads):
        outputs.append(
            window_attend(
                queries[:, :, :, head_index, :],
                window_keys[:, :, :, head_index, :],
                window_values[:, :, :, head_index, :],
                allowed,
            )
        )
    attended = jnp.stack(outputs, 3).reshape(token_count, group_heads * HD)
    gathered_out = lax.all_gather(out_weight, "tx", axis=1, tiled=True)
    own_rows = token_count // rep_devices
    own_hidden = lax.dynamic_slice_in_dim(flat_hidden, rep_place * own_rows, own_rows, 0)
    summed = lax.psum_scatter(
        jnp.dot(attended, gathered_out, preferred_element_type=jnp.float32).astype(jnp.bfloat16),
        "rep",
        scatter_dimension=0,
        tiled=True,
    ).astype(jnp.float32)
    result = (own_hidden.astype(jnp.float32) + summed).astype(jnp.bfloat16)
    return result.reshape(frame_count // rep_devices, tile_rows, tile_cols, model_width)


def solution(mesh):
    return jax.shard_map(
        body,
        mesh=mesh,
        in_specs=(
            P("tx", "ty", None, "rep"),
            P(("rep", "tx"), None),
            P("tx", "rep"),
            P("rep", "tx"),
            P(),
            P("ty", "tx", None),
        ),
        out_specs=P("rep", "ty", "tx", None),
        check_vma=False,
    )
```

profile of v0, /device:TPU:24, one launch (start us, length us, event | category | flops | bytes accessed | tf_op | source)
XLA Modules:
  0.0 499.9 jit_solution(13898322426307308354)
XLA Ops:
  8.3 28.7 %all_to_all.18 = bf16[1,2,32,768]{3,1,0,2:T(2,128)(2,1)S(1)} all-to-all(bf16[1,2,32,768]{3,1,0,2:T(2,128)(2,1)S(1)} %copy.62), channel_id=1, replica_groups=mesh['rep'=4,'ty'=8,'tx'=16] {'tx'}, dimensions={2} | all-to-all | bytes 196608 | tf_op jit(solution)/shard_map/all_to_all | solution.py:117
  37.1 4.5 collective-permute-start
  43.6 7.7 %collective-permute-done.1 = bf16[16,1,2,768]{3,2,1,0:T(2,128)(2,1)S(1)} collective-permute-done((bf16[16,1,2,768]{3,2,1,0:T(2,128)(2,1)S(1)}, bf16[16,1,2,768]{3,2,1,0:T(2,128)(2,1)S(1)}, u32[]{:S(2)}, u32[]{:S(2)}) %collective-permute-start.1) | collective-permute-done | bytes 49184 | tf_op jit(solution)/shard_map/ppermute | solution.py:25
  56.5 4.3 collective-permute-done.2
  65.8 24.4 %all-gather.3.cloned.1.call-done = bf16[768,1920]{1,0:T(8,128)(2,1)} async-done(((bf16[48,1920]{1,0:T(8,128)(2,1)}), bf16[768,1920]{1,0:T(8,128)(2,1)}) %all-gather.3.cloned.1.call-update) | async-done | bytes 2949136 | tf_op jit(solution)/shard_map/all_gather | solution.py:121
  99.1 66.1 %all-reduce.2.cloned.1.call-done = f32[16,4,4,1920]{3,1,2,0:T(4,128)} async-done(((f32[16,4,4,1920]{3,1,2,0:T(4,128)}), f32[16,4,4,1920]{3,1,2,0:T(4,128)}) %all-reduce.2.cloned.1.call-update) | async-done | bytes 1966096 | tf_op jit(solution)/shard_map/psum | solution.py:122
  167.3 5.2 %broadcast_select_fusion.1 = (f32[16,1,4,1920]{3,1,2,0:T(1,128)S(1)}, f32[16,1,4,1920]{3,1,2,0:T(1,128)S(1)}) fusion(pred[]{:T(512)S(6)} %eq.40, f32[16,4,4,1920]{3,1,2,0:T(4,128)} %all-reduce.2.cloned.1.call-done, pred[]{:T(512)S(6)} %eq.41), kind=kLoop, calls=%fused_computation.65 | loop fusion | flops 245760 | bytes 2949122 | tf_op jit(solution)/shard_map/jit(_where)/select_n | solution.py:51
  177.8 9.3 %multiply_reduce_fusion = (f32[16,8,8]{2,1,0:T(8,128)S(1)}, bf16[16,8,1920,8]{2,3,1,0:T(8,128)(2,1)}) fusion(f32[8]{0:T(128)S(1)} %broadcast_maximum_fusion, s32[8]{0:T(128)S(1)} %get-tuple-element.49, f32[8]{0:T(128)S(1)} %get-tuple-element.50, s32[8]{0:T(128)S(1)} %get-tuple-element.48, f32[8]{0:T(128)S(1)} %get-tuple-element.51, ...), kind=kOutput, calls=%fused_computation.5 | convolution fusion | flops 102235392 | bytes 7868608 | tf_op jit(solution)/shard_map/wq,fhqc->fhwc/dot_general | solution.py:133
  187.2 57.1 %all-gather.5.cloned.1.call-done = bf16[1920,768]{1,0:T(8,128)(2,1)} async-done(((bf16[120,768]{1,0:T(8,128)(2,1)}), bf16[1920,768]{1,0:T(8,128)(2,1)}) %all-gather.5.cloned.1.call-update) | async-done | bytes 2949136 | tf_op jit(solution)/shard_map/all_gather | solution.py:141
  244.4 6.5 %fusion.37 = bf16[1024,768]{1,0:T(8,128)(2,1)S(1)} fusion(bf16[1920,768]{1,0:T(8,128)(2,1)} %all-gather.5.cloned.1.call-done, bf16[1024,1920]{1,0:T(8,128)(2,1)} %bitcast.74, f32[1920]{0:T(1024)S(1)} %convert_element_type.85, f32[1024]{0:T(1024)S(1)} %rsqrt.12), kind=kOutput, calls=%fused_computation.57 | convolution fusion | flops 3028549632 | bytes 8465920 | tf_op jit(solution)/shard_map/dot_general | solution.py:107
  250.9 4.9 reshape.161
  255.8 19.8 %slice_reduce_fusion = (bf16[16,8,8,4,64]{4,3,2,1,0:T(4,128)(2,1)}, bf16[16,8,8,4,64]{4,3,2,1,0:T(4,128)(2,1)S(1)}, bf16[16,8,8,4,1,64]{5,4,3,2,1,0:T(2,128)(2,1)S(1)}) fusion(bf16[16,8,8,4,3,64]{5,4,3,2,1,0:T(4,128)(2,1)} %reshape.161), kind=kLoop, calls=%fused_computation.31 | loop fusion | bytes 3145728 | tf_op jit(solution)/shard_map/slice | solution.py:148
  283.5 4.8 collective-permute-start.4
  295.3 8.0 %collective-permute-done.5 = bf16[2,16,4,8,256]{4,3,2,1,0:T(8,128)(2,1)} collective-permute-done((bf16[2,16,4,8,256]{4,3,2,1,0:T(8,128)(2,1)}, bf16[2,16,4,8,256]{4,3,2,1,0:T(8,128)(2,1)}, u32[]{:S(2)}, u32[]{:S(2)}) %collective-permute-start.5) | collective-permute-done | bytes 524320 | tf_op jit(solution)/shard_map/ppermute | solution.py:25
  307.2 4.5 collective-permute-start.6
  313.2 46.7 %all_gather.11 = bf16[256,1920]{0,1:T(8,128)(2,1)} all-gather(bf16[256,120]{0,1:T(8,128)(2,1)S(1)} %copy-done.3), channel_id=1, replica_groups=mesh['rep'=4,'ty'=8,'tx'=16] {'tx'}, dimensions={1}, use_global_device_ids=true | all-gather | bytes 1044480 | tf_op jit(solution)/shard_map/all_gather | solution.py:179
  361.3 4.7 pad_maximum_fusion
  367.6 7.1 %reshape_squeeze.43 = bf16[16,16,16,4,64]{4,3,2,1,0:T(4,128)(2,1)} reshape(bf16[1,16,16,16,256]{4,3,2,1,0:T(8,128)(2,1)} %get-tuple-element.15) | data formatting | bytes 4194304 | tf_op jit(solution)/shard_map/reshape;squeeze | solution.py:153
  377.9 14.0 %fusion.82 = (bf16[16,16,16,1,64]{4,3,2,1,0:T(2,128)(2,1)S(1)}, bf16[16,16,16,1,64]{4,3,2,1,0:T(2,128)(2,1)S(1)}, bf16[16,16,16,1,64]{4,3,2,1,0:T(2,128)(2,1)S(1)}, bf16[16,16,16,1,64]{4,3,2,1,0:T(2,128)(2,1)S(1)}) fusion(bf16[16,16,16,4,64]{4,3,2,1,0:T(4,128)(2,1)} %reshape_squeeze.45), kind=kLoop, calls=%fused_computation.127 | loop fusion | bytes 4194304 | tf_op jit(solution)/shard_map/slice | solution.py:174
  394.9 7.9 %fusion.81 = (bf16[16,16,16,1,64]{4,3,2,1,0:T(2,128)(2,1)S(1)}, bf16[16,16,16,1,64]{4,3,2,1,0:T(2,128)(2,1)S(1)}, bf16[16,16,16,1,64]{4,3,2,1,0:T(2,128)(2,1)S(1)}, bf16[16,16,16,1,64]{4,3,2,1,0:T(2,128)(2,1)S(1)}) fusion(bf16[16,16,16,4,64]{4,3,2,1,0:T(4,128)(2,1)S(1)} %copy-done), kind=kLoop, calls=%fused_computation.126 | loop fusion | bytes 4194304 | tf_op jit(solution)/shard_map/slice | solution.py:173
  406.6 4.5 fusion.90
  414.6 4.6 fusion.92
  423.4 4.6 fusion.91
  444.4 46.1 %reduce-scatter.2.cloned.1.call-done = bf16[256,1920]{1,0:T(8,128)(2,1)} async-done(((bf16[1024,1920]{1,0:T(8,128)(2,1)}), bf16[256,1920]{1,0:T(8,128)(2,1)}) %reduce-scatter.2.cloned.1.call-update) | async-done | bytes 983056 | tf_op jit(solution)/shard_map/reduce_scatter | solution.py:182
  (90 shorter events, 87.4 us)
Async XLA Ops:
  6.5 83.7 %all-gather.3.cloned.1.call-start = ((), (), s32[]{:S(2)}) async-start(), calls=%async_computation.2 | async-start | bytes 3133440 | tf_op jit(solution)/shard_map/all_gather | solution.py:121
  7.3 158.0 %all-reduce.2.cloned.1.call-start = ((), (), s32[]{:S(2)}) async-start(), calls=%async_computation.3 | async-start | bytes 3932160 | tf_op jit(solution)/shard_map/psum | solution.py:122
  37.1 6.4 %collective-permute-start = (bf16[16,1,2,768]{3,2,1,0:T(2,128)(2,1)S(1)}, bf16[16,1,2,768]{3,2,1,0:T(2,128)(2,1)S(1)}, u32[]{:S(2)}, u32[]{:S(2)}) collective-permute-start(bf16[16,1,2,768]{3,2,1,0:T(2,128)(2,1)S(1)} %get-tuple-element.32), channel_id=1, source_target_pairs={{0,16},{16,32},{32,48},{48,64},{64,80},{80,96},{96,112},{1,17},{17... | collective-permute-start | bytes 147464 | tf_op jit(solution)/shard_map/ppermute | solution.py:23
  41.6 9.6 %collective-permute-start.1 = (bf16[16,1,2,768]{3,2,1,0:T(2,128)(2,1)S(1)}, bf16[16,1,2,768]{3,2,1,0:T(2,128)(2,1)S(1)}, u32[]{:S(2)}, u32[]{:S(2)}) collective-permute-start(bf16[16,1,2,768]{3,2,1,0:T(2,128)(2,1)S(1)} %get-tuple-element.33), channel_id=1, source_target_pairs={{16,0},{32,16},{48,32},{64,48},{80,64},{96,80},{112,96},{17,1},{33... | collective-permute-start | bytes 147464 | tf_op jit(solution)/shard_map/ppermute | solution.py:25
  51.8 9.1 %collective-permute-start.2 = (bf16[16,4,1,768]{3,2,1,0:T(2,128)(2,1)S(1)}, bf16[16,4,1,768]{3,2,1,0:T(2,128)(2,1)S(1)}, u32[]{:S(2)}, u32[]{:S(2)}) collective-permute-start(bf16[16,4,1,768]{3,2,1,0:T(2,128)(2,1)S(1)} %get-tuple-element.30), channel_id=1, source_target_pairs={{0,1},{1,2},{2,3},{3,4},{4,5},{5,6},{6,7},{7,8},{8,9},{9,10},{10,1... | collective-permute-start | bytes 294920 | tf_op jit(solution)/shard_map/ppermute | solution.py:23
  55.2 9.8 %collective-permute-start.3 = (bf16[16,4,1,768]{3,2,1,0:T(2,128)(2,1)S(1)}, bf16[16,4,1,768]{3,2,1,0:T(2,128)(2,1)S(1)}, u32[]{:S(2)}, u32[]{:S(2)}) collective-permute-start(bf16[16,4,1,768]{3,2,1,0:T(2,128)(2,1)S(1)} %get-tuple-element.31), channel_id=1, source_target_pairs={{1,0},{2,1},{3,2},{4,3},{5,4},{6,5},{7,6},{8,7},{9,8},{10,9},{11,1... | collective-permute-start | bytes 294920 | tf_op jit(solution)/shard_map/ppermute | solution.py:25
  94.3 4.8 copy-start.5
  98.1 146.3 %all-gather.5.cloned.1.call-start = ((), (), s32[]{:S(2)}) async-start(), calls=%async_computation.4 | async-start | bytes 3133440 | tf_op jit(solution)/shard_map/all_gather | solution.py:141
  98.8 391.7 %reduce-scatter.2.cloned.1.call-start = ((), (), s32[]{:S(2)}) async-start(), calls=%async_computation.5 | async-start | bytes 4915200 | tf_op jit(solution)/shard_map/reduce_scatter | solution.py:182
  275.6 14.6 %copy-start.4 = (s32[1,1,4]{2,1,0:T(1,128)S(1)}, s32[1,1,4]{2,1,0:T(1,128)}, u32[]{:S(2)}) copy-start(s32[1,1,4]{2,1,0:T(1,128)} %param.11) | copy-start | bytes 52
  283.5 11.8 %collective-permute-start.4 = (bf16[2,16,4,8,256]{4,3,2,1,0:T(8,128)(2,1)}, bf16[2,16,4,8,256]{4,3,2,1,0:T(8,128)(2,1)}, u32[]{:S(2)}, u32[]{:S(2)}) collective-permute-start(bf16[2,16,4,8,256]{4,3,2,1,0:T(8,128)(2,1)} %get-tuple-element.28), channel_id=1, source_target_pairs={{0,16},{16,32},{32,48},{48,64},{64,80},{80,96},{96,112},{1,17},{17... | collective-permute-start | bytes 1572872 | tf_op jit(solution)/shard_map/ppermute | solution.py:23
  288.3 15.0 %collective-permute-start.5 = (bf16[2,16,4,8,256]{4,3,2,1,0:T(8,128)(2,1)}, bf16[2,16,4,8,256]{4,3,2,1,0:T(8,128)(2,1)}, u32[]{:S(2)}, u32[]{:S(2)}) collective-permute-start(bf16[2,16,4,8,256]{4,3,2,1,0:T(8,128)(2,1)} %get-tuple-element.29), channel_id=1, source_target_pairs={{16,0},{32,16},{48,32},{64,48},{80,64},{96,80},{112,96},{17,1},{33... | collective-permute-start | bytes 1572872 | tf_op jit(solution)/shard_map/ppermute | solution.py:25
  293.3 19.8 %copy-start.3 = (bf16[256,120]{0,1:T(8,128)(2,1)S(1)}, bf16[256,120]{0,1:T(8,128)(2,1)}, u32[]{:S(2)}) copy-start(bf16[256,120]{0,1:T(8,128)(2,1)} %param.9) | copy-start | bytes 184324
  307.2 54.1 %collective-permute-start.6 = (bf16[2,16,16,4,256]{4,3,2,1,0:T(4,128)(2,1)}, bf16[2,16,16,4,256]{4,3,2,1,0:T(4,128)(2,1)}, u32[]{:S(2)}, u32[]{:S(2)}) collective-permute-start(bf16[2,16,16,4,256]{4,3,2,1,0:T(4,128)(2,1)} %get-tuple-element.18), channel_id=1, source_target_pairs={{0,1},{1,2},{2,3},{3,4},{4,5},{5,6},{6,7},{7,8},{8,9},{9,10},{10,1... | collective-permute-start | bytes 3145736 | tf_op jit(solution)/shard_map/ppermute | solution.py:23
  311.7 49.6 %collective-permute-start.7 = (bf16[2,16,16,4,256]{4,3,2,1,0:T(4,128)(2,1)}, bf16[2,16,16,4,256]{4,3,2,1,0:T(4,128)(2,1)}, u32[]{:S(2)}, u32[]{:S(2)}) collective-permute-start(bf16[2,16,16,4,256]{4,3,2,1,0:T(4,128)(2,1)} %get-tuple-element.19), channel_id=1, source_target_pairs={{1,0},{2,1},{3,2},{4,3},{5,4},{6,5},{7,6},{8,7},{9,8},{10,9},{11,1... | collective-permute-start | bytes 3145736 | tf_op jit(solution)/shard_map/ppermute | solution.py:25
  392.1 2.8 copy-start
  435.5 3.2 copy-start.2
  438.5 2.6 copy-start.1
Sparse Core Ops, SparseCore 0:
  9.4 80.7 all-gather.2
  98.2 67.0 all-reduce.1
  167.4 76.9 all-gather.4
  444.5 45.9 reduce-scatter.1
where the time goes:
time: 506 us; the launch traced here: 500 us
  waiting for transfers between devices  221 us (44%)
  local copies, waits for them, and re-layouts  88.6 us (18%)
  blocking collectives  75.4 us (15%)
  matrix products  57.5 us (11%)
  starting transfers between devices  23.9 us (5%)
  other arithmetic  16.9 us (3%)
  between operations  16.2 us (3%)
    psum x1, waiting for transfers between devices, body(): lax.psum(coarse, 'rep').reshape(frame_count, coarse_rows, coarse_cols, -1)  66.1 us
    all_gather x1, waiting for transfers between devices, body(): lax.all_gather(qkv_weight, 'tx', axis=0, tiled=True)  57.1 us
    all_gather x1, blocking collectives, body(): gathered_out = lax.all_gather(out_weight, 'tx', axis=1, tiled=True)  46.7 us
    reduce_scatter x1, waiting for transfers between devices, body(): lax.psum_scatter(jnp.dot(attended, gathered_out, preferred_element_type=j...  46.1 us
    all_to_all x1, blocking collectives, body(): lax.all_to_all(latent, 'tx', split_axis=2, concat_axis=0, tiled=True)  28.7 us
    all_gather x1, waiting for transfers between devices, body(): lax.all_gather(in_weight, 'tx', axis=0, tiled=True)  24.4 us
    ppermute x4, waiting for transfers between devices, padded(): lax.ppermute(head, axis, [((i + 1) % count, i) for i in range(ends)])  19.8 us
    slice x1, local copies, waits for them, and re-layouts, body(): project[:, :, :, :, 2, :]  19.8 us
  transfers between devices with their start and end apart: 12, of which 9 were waited for; matrix products, arithmetic and copies ran while one was open for 5% of the time, Pallas kernels for 0%

commit v1 on v0

v1 whole, which is shorter than its diff:
```python
import jax
import jax.numpy as jnp
from jax import lax
from jax.experimental import pallas as pl
from jax.experimental.pallas import tpu as pltpu
from jax.sharding import PartitionSpec as P

HD = 64
U = 4
R = 4
CHUNKS = 16
CHUNK = 120
LANES = 128
WIDE = CHUNKS * LANES
WIDTH = CHUNKS * CHUNK
CELLS = 48
PATCH = 3 * CELLS
NEG = -1e30
F32 = jnp.float32
BF16 = jnp.bfloat16


def call(kernel, out_shape, vmem_mb, **kw):
    return pl.pallas_call(
        kernel,
        out_shape=out_shape,
        compiler_params=pltpu.CompilerParams(vmem_limit_bytes=vmem_mb << 20),
        **kw,
    )


def bridge_kernel(cells_ref, moved_ref, out_ref, weight_ref):
    for t in range(16):
        for b in range(3):
            weight_ref[t * 48 + b * 16 : t * 48 + b * 16 + 16, :] = moved_ref[
                t, 0:16, b * 256 : (b + 1) * 256
            ]
    sums = jnp.dot(cells_ref[...], weight_ref[...], preferred_element_type=F32).astype(BF16)
    for y in range(8):
        for dy in range(3):
            source = min(max(y + dy - 1, 0), 7)
            for r in range(4):
                start = source * 64 + r * 16
                out_ref[r, y, dy] = sums[start : start + 16, :]


def reduce_kernel(parts_ref, gain_ref, coarse_ref, gained_ref):
    for y in range(8):
        total = parts_ref[y].astype(F32)
        for r in range(1, 4):
            total = total + parts_ref[r * 8 + y].astype(F32)
        lanes = slice(y * 256, (y + 1) * 256)
        coarse_ref[:, lanes] = total.astype(BF16)
        gained_ref[:, lanes] = (total * gain_ref[:, lanes]).astype(BF16)


def project_kernel(gained_ref, weights_ref, project_ref, out_weight_ref):
    total = jnp.zeros(project_ref.shape, F32)
    for t in range(CHUNKS):
        total = total + jnp.dot(
            gained_ref[:, t * LANES : (t + 1) * LANES],
            weights_ref[t, 48:176, :],
            preferred_element_type=F32,
        )
    project_ref[...] = total.astype(BF16)
    for t in range(CHUNKS):
        for b in range(6):
            rows = 48 if b < 5 else 16
            out_weight_ref[t, b * 48 : b * 48 + rows, :] = weights_ref[
                t, 0:rows, b * LANES : (b + 1) * LANES
            ]


def axis_weight(fine, cell, low, high):
    near = ((fine + 4) >> 2) - 1
    offset = ((fine + 4) & 3).astype(F32) * 0.25 - 0.375
    before = jnp.clip(near - 1, low, high)
    after = jnp.clip(near + 1, low, high)
    return (
        jnp.where(cell == near, 1.0 - jnp.abs(offset), 0.0)
        + jnp.where(cell == before, jnp.maximum(-offset, 0.0), 0.0)
        + jnp.where(cell == after, jnp.maximum(offset, 0.0), 0.0)
    )


def patch_matrix(frame, fine_row, fine_col, tokens, ty, tx):
    lane = lax.broadcasted_iota(jnp.int32, (tokens, PATCH), 1)
    piece = (lane >= CELLS).astype(jnp.int32) + (lane >= 2 * CELLS).astype(jnp.int32)
    rest = lane - piece * CELLS
    row = ((rest >> 4) << 1) + ((rest >> 1) & 1) - 2
    col = (piece << 1) + (rest & 1) - 2
    weight = axis_weight(fine_row, row, -2 * ty, 15 - 2 * ty) * axis_weight(
        fine_col, col, -2 * tx, 31 - 2 * tx
    )
    return jnp.where(((rest >> 2) & 3) == frame, weight, 0.0).astype(BF16)


def norm_kernel(
    place_ref, left_ref, own_ref, right_ref, keys_ref, query_ref, key_scale_ref, query_scale_ref, bias_ref, hidden_ref
):
    ty, tx = place_ref[0], place_ref[1]
    patch = jnp.concatenate([left_ref[...], own_ref[...], right_ref[...]], axis=0)

    def scale_of(field):
        wide = field.astype(F32)
        return lax.rsqrt(jnp.sum(wide * wide, axis=1, keepdims=True) * (1.0 / WIDTH) + 1e-06)

    token = lax.broadcasted_iota(jnp.int32, (256, PATCH), 0)
    for frame in range(4):
        matrix = patch_matrix(frame, (token >> 4) - R, (token & 15) - R, 256, ty, tx)
        rows = slice(frame * 256, (frame + 1) * 256)
        keys_ref[rows, :] = matrix
        field = jnp.dot(matrix, patch, preferred_element_type=F32).astype(BF16)
        key_scale_ref[rows, :] = jnp.broadcast_to(scale_of(field), (256, LANES))
    matrix = patch_matrix(token >> 6, (token >> 3) & 7, token & 7, 256, ty, tx)
    query_ref[...] = matrix
    hidden = jnp.dot(matrix, patch, preferred_element_type=F32).astype(BF16)
    hidden_ref[...] = hidden
    query_scale_ref[...] = jnp.broadcast_to(scale_of(hidden), (256, LANES))
    place = lax.broadcasted_iota(jnp.int32, (1024, LANES), 0)
    row = ((place >> 4) & 15) - R
    col = (place & 15) - R
    allowed = (
        (row + 8 * ty >= 0)
        & (row + 8 * ty < 64)
        & (row >= -place_ref[2])
        & (row < 8 + place_ref[3])
        & (col + 8 * tx >= 0)
        & (col + 8 * tx < 128)
        & (col >= -place_ref[4])
        & (col < 8 + place_ref[5])
    )
    bias_ref[...] = jnp.where(allowed, 0.0, NEG)


def attend_kernel(
    left_ref, own_ref, right_ref, keys_ref, query_ref, key_scale_ref, query_scale_ref, bias_ref, out_ref
):
    patch = jnp.concatenate([left_ref[0], own_ref[0], right_ref[0]], axis=0)
    fine = jnp.dot(keys_ref[...], patch, preferred_element_type=F32)
    scale = key_scale_ref[...]
    bias = bias_ref[...]
    first = fine[:, 0:128] * scale
    second = fine[:, 128:256] * scale
    third = fine[:, 256:384] * scale
    lane = lax.broadcasted_iota(jnp.int32, (1024, LANES), 1)
    low = lane < HD
    key_0 = jnp.where(low, jnp.where(lane == 0, bias, 0.0), first).astype(BF16)
    value_0 = jnp.where(low, second, 1.0).astype(BF16)
    key_1 = jnp.where(low, third, jnp.where(lane == HD, bias, 0.0)).astype(BF16)
    value_1 = jnp.where(low, 1.0, third).astype(BF16)
    query = jnp.dot(query_ref[...], patch[:, 0:256], preferred_element_type=F32)
    query_scale = query_scale_ref[...] * (HD ** (-0.5) * 1.4426950408889634)
    query_lane = lax.broadcasted_iota(jnp.int32, (256, LANES), 1)
    query_low = query_lane < HD
    turned_0 = pltpu.roll(query[:, 0:128] * query_scale, HD, 1)
    turned_1 = pltpu.roll(query[:, 128:256] * query_scale, HD, 1)
    query_0 = jnp.where(query_low, jnp.where(query_lane == 0, 1.0, 0.0), turned_0).astype(BF16)
    query_1 = jnp.where(query_low, turned_1, jnp.where(query_lane == HD, 1.0, 0.0)).astype(BF16)

    def head(q, k, v):
        scores = lax.dot_general(q, k, (((1,), (1,)), ((), ())), preferred_element_type=F32)
        weights = jnp.exp2(scores - jnp.max(scores, axis=1, keepdims=True)).astype(BF16)
        return jnp.dot(weights, v, preferred_element_type=F32)

    mixed_0 = head(query_0, key_0, value_0)
    mixed_1 = head(query_1, key_1, value_1)
    mixed = jnp.where(query_low, mixed_0 / mixed_0[:, HD : HD + 1], mixed_1 / mixed_1[:, 0:1])
    out_ref[0] = mixed.astype(BF16)


def output_kernel(place_ref, attended_ref, hidden_ref, w0_ref, w1_ref, w2_ref, w3_ref, out_ref):
    rep = place_ref[0]
    weights = (w0_ref, w1_ref, w2_ref, w3_ref)
    groups = [attended_ref[rep ^ k] for k in range(4)]
    chunks = []
    for t in range(0, CHUNKS, 2):
        total = hidden_ref[:, t * LANES : (t + 2) * LANES].astype(F32)
        for k in range(4):
            pair = jnp.concatenate([weights[k][t], weights[k][t + 1]], axis=1)
            total = total + jnp.dot(groups[k], pair, preferred_element_type=F32)
        chunks.append(total[:, 0:LANES])
        chunks.append(total[:, LANES : 2 * LANES])
    lane = lax.broadcasted_iota(jnp.int32, (256, LANES), 1)
    for j in range(15):
        here, shift = chunks[j], (LANES - 8 * j) % LANES
        if shift:
            here = pltpu.roll(here, shift, 1)
        after = pltpu.roll(chunks[j + 1], CHUNK - 8 * j, 1)
        out_ref[:, j * LANES : (j + 1) * LANES] = jnp.where(lane < CHUNK - 8 * j, here, after).astype(BF16)


def body(latent, in_weight, qkv_weight, out_weight, norm_gain, extents):
    ty = lax.axis_index("ty")
    tx = lax.axis_index("tx")
    rep = lax.axis_index("rep")
    smem = pl.BlockSpec(memory_space=pltpu.SMEM)

    out_rows = jnp.pad(out_weight, ((0, 32), (0, LANES - CHUNK))).reshape(6, 48, LANES)
    shard = jnp.concatenate(
        [out_rows.transpose(1, 0, 2).reshape(48, 768), qkv_weight, jnp.zeros((8, 768), BF16)], axis=0
    )
    gathered = lax.all_gather(shard, "tx", axis=0)

    source = lax.broadcasted_iota(jnp.int32, (WIDTH, 256), 0)
    target = lax.broadcasted_iota(jnp.int32, (WIDTH, 256), 1)
    inside = target & 127
    pick = ((inside < CHUNK) & (source == ty * 240 + (target >> 7) * CHUNK + inside)).astype(BF16)
    columns = jnp.dot(in_weight, pick, preferred_element_type=F32).astype(BF16)
    columns = columns.reshape(3, 16, 256).transpose(1, 0, 2).reshape(1, 16, 768)
    tiles = latent.reshape(2, 16, 2, 768).transpose(1, 0, 2, 3).reshape(16, 4, 768)
    message = jnp.concatenate([jnp.broadcast_to(columns, (16, 16, 768)), tiles], axis=1)
    moved = lax.all_to_all(message, "tx", split_axis=0, concat_axis=0, tiled=True)
    cells = moved[:, 16:20, :].reshape(1, 64, 768)
    cells = lax.all_to_all(jnp.broadcast_to(cells, (8, 64, 768)), "ty", split_axis=0, concat_axis=0, tiled=True)
    sums = call(
        bridge_kernel,
        jax.ShapeDtypeStruct((4, 8, 3, 16, 256), BF16),
        16,
        scratch_shapes=[pltpu.VMEM((768, 256), BF16)],
    )(cells.reshape(512, 768), moved)
    parts = lax.all_to_all(
        sums.reshape(32, CELLS, 256), ("rep", "ty"), split_axis=0, concat_axis=0, tiled=True
    )
    gain = jnp.pad(norm_gain.astype(F32).reshape(CHUNKS, CHUNK), ((0, 0), (0, LANES - CHUNK))).reshape(1, WIDE)
    coarse, gained = call(
        reduce_kernel, [jax.ShapeDtypeStruct((CELLS, WIDE), BF16)] * 2, 16
    )(parts, gain)

    count = lax.axis_size("tx")
    to_right = [(i, i + 1) for i in range(count - 1)]
    to_left = [(i + 1, i) for i in range(count - 1)]
    coarse_left = lax.ppermute(coarse, "tx", to_right)
    coarse_right = lax.ppermute(coarse, "tx", to_left)
    gained = lax.all_gather(gained, "rep", axis=0, tiled=True)
    project, own_rows = call(
        project_kernel,
        [jax.ShapeDtypeStruct((4 * CELLS, 768), BF16), jax.ShapeDtypeStruct((CHUNKS, 256, LANES), BF16)],
        32,
    )(gained, gathered)
    project = lax.all_to_all(
        project.reshape(4, CELLS, 768), "rep", split_axis=0, concat_axis=0, tiled=True
    )
    project_left = lax.ppermute(project, "tx", to_right)
    project_right = lax.ppermute(project, "tx", to_left)

    far_rows = lax.ppermute(own_rows, "rep", [(i, i ^ 2) for i in range(4)])
    near_rows = lax.ppermute(own_rows, "rep", [(i, i ^ 1) for i in range(4)])
    last_rows = lax.ppermute(far_rows, "rep", [(i, i ^ 1) for i in range(4)])

    place = jnp.concatenate([jnp.stack([ty, tx]).astype(jnp.int32), extents.reshape(4)])
    vmem = pl.BlockSpec(memory_space=pltpu.VMEM)
    keys, query, key_scale, query_scale, bias, hidden = call(
        norm_kernel,
        [
            jax.ShapeDtypeStruct((1024, PATCH), BF16),
            jax.ShapeDtypeStruct((256, PATCH), BF16),
            jax.ShapeDtypeStruct((1024, LANES), F32),
            jax.ShapeDtypeStruct((256, LANES), F32),
            jax.ShapeDtypeStruct((1024, LANES), F32),
            jax.ShapeDtypeStruct((256, WIDE), BF16),
        ],
        32,
        in_specs=[smem, vmem, vmem, vmem],
        out_specs=[vmem] * 6,
    )(place, coarse_left, coarse, coarse_right)

    piece = pl.BlockSpec((1, CELLS, 384), lambda p: (p // 2, 0, p % 2))

    def whole(shape):
        return pl.BlockSpec(shape, lambda p: (0, 0))

    attended = call(
        attend_kernel,
        jax.ShapeDtypeStruct((4, 256, 256), BF16),
        32,
        grid=(8,),
        in_specs=[
            piece,
            piece,
            piece,
            whole((1024, PATCH)),
            whole((256, PATCH)),
            whole((1024, LANES)),
            whole((256, LANES)),
            whole((1024, LANES)),
        ],
        out_specs=pl.BlockSpec((1, 256, LANES), lambda p: (p // 2, 0, p % 2)),
    )(project_left, project, project_right, keys, query, key_scale, query_scale, bias)

    result = call(
        output_kernel,
        jax.ShapeDtypeStruct((256, WIDTH), BF16),
        32,
        in_specs=[smem] + [vmem] * 6,
        out_specs=vmem,
    )(rep.astype(jnp.int32).reshape(1), attended, hidden, own_rows, near_rows, far_rows, last_rows)
    return result.reshape(4, 8, 8, WIDTH)


def solution(mesh):
    return jax.shard_map(
        body,
        mesh=mesh,
        in_specs=(
            P("tx", "ty", None, "rep"),
            P(("rep", "tx"), None),
            P("tx", "rep"),
            P("rep", "tx"),
            P(),
            P("ty", "tx", None),
        ),
        out_specs=P("rep", "ty", "tx", None),
        check_vma=False,
    )
```

time: 506 us -> 204 us (0.40)
  waiting for transfers between devices: 221 us -> 51.6 us
  local copies, waits for them, and re-layouts: 88.6 us -> 4.63 us
  matrix products: 57.5 us -> 0.52 us
  Pallas kernels: 0 us -> 25.6 us
  other arithmetic: 16.9 us -> 1.9 us
  blocking collectives: 75.4 us -> 80.9 us
    all_gather x2 -> x1, waiting for transfers between devices: 81.6 us -> 0.01 us  [body(): gathered = lax.all_gather(shard, 'tx', axis=0)]
    psum x1 -> x0, waiting for transfers between devices: 66.1 us -> none  [body(): lax.psum(coarse, 'rep').reshape(frame_count, coarse_rows, coarse_cols, -1)]
    slice x13 -> x1, local copies, waits for them, and re-layouts: 51.3 us -> 0.03 us  [body(): cells = moved[:, 16:20, :].reshape(1, 64, 768)]
    reduce_scatter x1 -> x0, waiting for transfers between devices: 46.1 us -> none  [body(): lax.psum_scatter(jnp.dot(attended, gathered_out, preferred_element_type=j...]
    all_to_all x1 -> x2, blocking collectives: 28.7 us -> 72.4 us  [the longest x1 56.4 us: body(): lax.all_to_all(message, 'tx', split_axis=0, concat_axis=0, tiled=True)]
    dot_general x9 -> x1, matrix products: 39.4 us -> 0.52 us  [body(): columns = jnp.dot(in_weight, pick, preferred_element_type=F32).astype(BF16)]
    all_gather x1, blocking collectives: 46.7 us -> 8.45 us  [body(): gained = lax.all_gather(gained, 'rep', axis=0, tiled=True)]
    pallas_call x0 -> x6, Pallas kernels: none -> 25.6 us  [the longest x1 13.6 us: body(): call(attend_kernel, jax.ShapeDtypeStruct((4, 256, 256), BF16), 32, grid=(...]
  transfers between devices with their start and end apart: 12 -> 10, of which waited for: 9 -> 4; matrix products, arithmetic and copies ran while one was open for 5% -> 1% of each run, Pallas kernels for 0% -> 10%
where the time goes in v1:
time: 204 us; the launch traced here: 202 us
  blocking collectives  80.9 us (40%)
  waiting for transfers between devices  51.6 us (25%)
  Pallas kernels  25.6 us (13%)
  starting transfers between devices  23 us (11%)
  between operations  13.7 us (7%)
  local copies, waits for them, and re-layouts  4.63 us (2%)
    all_to_all x1, blocking collectives, body(): lax.all_to_all(message, 'tx', split_axis=0, concat_axis=0, tiled=True)  56.4 us
    ppermute x1, waiting for transfers between devices, body(): far_rows = lax.ppermute(own_rows, 'rep', [(i, i ^ 2) for i in range(4)])  22.5 us
    all_to_all x1, blocking collectives, body(): lax.all_to_all(jnp.broadcast_to(cells, (8, 64, 768)), 'ty', split_axis=0,...  16.1 us
    pallas_call x1, Pallas kernels, body(): call(attend_kernel, jax.ShapeDtypeStruct((4, 256, 256), BF16), 32, grid=(...  13.6 us
    ppermute x1, waiting for transfers between devices, body(): coarse_right = lax.ppermute(coarse, 'tx', to_left)  12.6 us
    all_to_all x1, waiting for transfers between devices, body(): lax.all_to_all(sums.reshape(32, CELLS, 256), ('rep', 'ty'), split_axis=0,...  12.2 us
    all_gather x1, blocking collectives, body(): gained = lax.all_gather(gained, 'rep', axis=0, tiled=True)  8.45 us
    all_to_all x1, starting transfers between devices, body(): lax.all_to_all(sums.reshape(32, CELLS, 256), ('rep', 'ty'), split_axis=0,...  5.99 us
  transfers between devices with their start and end apart: 10, of which 4 were waited for; matrix products, arithmetic and copies ran while one was open for 1% of the time, Pallas kernels for 10%

profile of v1, /device:TPU:24, one launch (start us, length us, event | category | flops | bytes accessed | tf_op | source)
XLA Modules:
  0.0 201.8 jit_solution(17099602969740646633)
XLA Ops:
  6.5 1.0 copy.12
  7.7 1.7 maximum_maximum_fusion
  11.2 56.4 %all_to_all.20.moved_ref = bf16[16,20,768]{2,1,0:T(8,128)(2,1)S(1)} all-to-all(bf16[16,20,768]{2,1,0:T(8,128)(2,1)S(1)} %pad_maximum_fusion), channel_id=1, replica_groups=mesh['rep'=4,'ty'=8,'tx'=16] {'tx'}, dimensions={0} | all-to-all | bytes 983040 | tf_op jit(solution)/shard_map/all_to_all | solution.py:213
  67.7 16.1 %all_to_all.21 = bf16[8,64,768]{2,1,0:T(8,128)(2,1)S(1)} all-to-all(bf16[8,64,768]{2,1,0:T(8,128)(2,1)S(1)} %broadcast_in_dim.20), channel_id=1, replica_groups=mesh['rep'=4,'ty'=8,'tx'=16] {'ty'}, dimensions={0} | all-to-all | bytes 1572864 | tf_op jit(solution)/shard_map/all_to_all | solution.py:215
  83.8 1.3 shard_map.64
  85.0 6.0 %all-to-all-start.2 = ((bf16[32,48,256]{2,1,0:T(8,128)(2,1)}), bf16[32,48,256]{2,1,0:T(8,128)(2,1)S(1)}, u32[]{:S(2)}, u32[]{:S(2)}) async-start(bf16[32,48,256]{2,1,0:T(8,128)(2,1)} %bitcast.6), calls=%async_computation.2 | async-start | bytes 1572864 | tf_op jit(solution)/shard_map/all_to_all | solution.py:222
  91.2 12.2 %all-to-all-done.2.parts_ref = bf16[32,48,256]{2,1,0:T(8,128)(2,1)S(1)} async-done(((bf16[32,48,256]{2,1,0:T(8,128)(2,1)}), bf16[32,48,256]{2,1,0:T(8,128)(2,1)S(1)}, u32[]{:S(2)}, u32[]{:S(2)}) %all-to-all-start.2) | async-done | bytes 786464 | tf_op jit(solution)/shard_map/all_to_all | solution.py:222
  104.2 8.4 %all_gather.9.gained_ref = bf16[192,2048]{1,0:T(8,128)(2,1)S(1)} all-gather(bf16[48,2048]{1,0:T(8,128)(2,1)S(1)} %get-tuple-element.15), channel_id=1, replica_groups=mesh['rep'=4,'ty'=8,'tx'=16] {'rep'}, dimensions={0}, use_global_device_ids=true | all-gather | bytes 983040 | tf_op jit(solution)/shard_map/all_gather | solution.py:235
  112.6 2.2 %copy-done.1 = bf16[2816,768]{1,0:T(8,128)(2,1)S(1)} copy-done((bf16[2816,768]{1,0:T(8,128)(2,1)S(1)}, bf16[2816,768]{1,0:T(8,128)(2,1)}, u32[]{:S(2)}) %copy-start.1) | copy-done | bytes 4325400
  114.9 2.2 %shard_map.66 = (bf16[192,768]{1,0:T(8,128)(2,1)}, bf16[16,256,128]{2,1,0:T(8,128)(2,1)S(1)}) custom-call(bf16[192,2048]{1,0:T(8,128)(2,1)S(1)} %all_gather.9.gained_ref, bf16[16,176,768]{2,1,0:T(8,128)(2,1)S(1)} %bitcast.29), custom_call_target="tpu_custom_call" | custom-call | tf_op jit(solution)/shard_map/pallas_call | solution.py:236
  117.1 2.9 %collective-permute-start.5 = (bf16[16,256,128]{2,1,0:T(8,128)(2,1)S(1)}, bf16[16,256,128]{2,1,0:T(8,128)(2,1)S(1)}, u32[]{:S(2)}, u32[]{:S(2)}) collective-permute-start(bf16[16,256,128]{2,1,0:T(8,128)(2,1)S(1)} %get-tuple-element.24.w0_ref), channel_id=1, source_target_pairs={{0,256},{128,384},{256,0},{384,128},{1,257},{129,385},{257,1},{385... | collective-permute-start | bytes 3145736 | tf_op jit(solution)/shard_map/ppermute | solution.py:247
  119.9 1.9 collective-permute-start.4
  121.9 22.5 %collective-permute-done.5.w2_ref = bf16[16,256,128]{2,1,0:T(8,128)(2,1)S(1)} collective-permute-done((bf16[16,256,128]{2,1,0:T(8,128)(2,1)S(1)}, bf16[16,256,128]{2,1,0:T(8,128)(2,1)S(1)}, u32[]{:S(2)}, u32[]{:S(2)}) %collective-permute-start.5) | collective-permute-done | bytes 1048608 | tf_op jit(solution)/shard_map/ppermute | solution.py:247
  144.4 1.9 collective-permute-start.6
  146.3 3.5 %all-to-all-start.3 = ((bf16[4,48,768]{2,1,0:T(8,128)(2,1)}), bf16[4,48,768]{2,1,0:T(8,128)(2,1)S(1)}, u32[]{:S(2)}, u32[]{:S(2)}) async-start(bf16[4,48,768]{2,1,0:T(8,128)(2,1)} %bitcast.11), calls=%async_computation.3 | async-start | bytes 589824 | tf_op jit(solution)/shard_map/all_to_all | solution.py:241
  149.7 2.1 %collective-permute-start.2 = (bf16[48,2048]{1,0:T(8,128)(2,1)}, bf16[48,2048]{1,0:T(8,128)(2,1)S(1)}, u32[]{:S(2)}, u32[]{:S(2)}) collective-permute-start(bf16[48,2048]{1,0:T(8,128)(2,1)} %get-tuple-element.17.own_ref), channel_id=1, source_target_pairs={{0,1},{1,2},{2,3},{3,4},{4,5},{5,6},{6,7},{7,8},{8,9},{9,10},{10,1... | collective-permute-start | bytes 589832 | tf_op jit(solution)/shard_map/ppermute | solution.py:233
  151.9 4.2 %all-to-all-done.3.own_ref = bf16[4,48,768]{2,1,0:T(8,128)(2,1)S(1)} async-done(((bf16[4,48,768]{2,1,0:T(8,128)(2,1)}), bf16[4,48,768]{2,1,0:T(8,128)(2,1)S(1)}, u32[]{:S(2)}, u32[]{:S(2)}) %all-to-all-start.3) | async-done | bytes 294944 | tf_op jit(solution)/shard_map/all_to_all | solution.py:241
  156.1 2.1 %collective-permute-start = (bf16[4,48,768]{2,1,0:T(8,128)(2,1)S(1)}, bf16[4,48,768]{2,1,0:T(8,128)(2,1)S(1)}, u32[]{:S(2)}, u32[]{:S(2)}) collective-permute-start(bf16[4,48,768]{2,1,0:T(8,128)(2,1)S(1)} %all-to-all-done.3.own_ref), channel_id=1, source_target_pairs={{0,1},{1,2},{2,3},{3,4},{4,5},{5,6},{6,7},{7,8},{8,9},{9,10},{10,1... | collective-permute-start | bytes 884744 | tf_op jit(solution)/shard_map/ppermute | solution.py:244
  158.2 1.3 collective-permute-start.1
  159.5 1.3 collective-permute-start.3
  160.9 12.6 %collective-permute-done.3.right_ref = bf16[48,2048]{1,0:T(8,128)(2,1)} collective-permute-done((bf16[48,2048]{1,0:T(8,128)(2,1)}, bf16[48,2048]{1,0:T(8,128)(2,1)}, u32[]{:S(2)}, u32[]{:S(2)}) %collective-permute-start.3) | collective-permute-done | bytes 196640 | tf_op jit(solution)/shard_map/ppermute | solution.py:234
  173.6 3.9 %shard_map.67 = (bf16[1024,144]{1,0:T(8,128)(2,1)S(1)}, bf16[256,144]{1,0:T(8,128)(2,1)S(1)}, f32[1024,128]{1,0:T(8,128)S(1)}, f32[256,128]{1,0:T(8,128)S(1)}, f...) custom-call(s32[6]{0:T(128)S(1)} %pad_add_fusion.place_ref, bf16[48,2048]{1,0:T(8,128)(2,1)S(1)} %collective-permute-done.2.left_ref, ...), custom_call_target="tpu_custom_call" | custom-call | tf_op jit(solution)/shard_map/pallas_call | solution.py:253
  177.5 13.6 %shard_map.68.attended_ref = bf16[4,256,256]{2,1,0:T(8,128)(2,1)S(1)} custom-call(bf16[4,48,768]{2,1,0:T(8,128)(2,1)S(1)} %collective-permute-done.left_ref, bf16[4,48,768]{2,1,0:T(8,128)(2,1)S(1)} %all-to-all-done.3.own_ref, bf16[4,48,768]{2,1,0:T(8,128)(2,1)S(1)} %collective-permute-done.1.right_ref, bf16[1024,144]{1,0:T(8,128)(2,1)S(1)} %get-tuple-element.18.keys_ref, ...), custom_call_target="tpu_custom_call" | custom-call | tf_op jit(solution)/shard_map/pallas_call | solution.py:273
  191.1 3.8 %shard_map.69 = bf16[256,1920]{1,0:T(8,128)(2,1)} custom-call(s32[1]{0:T(128)} %bitcast.place_ref, bf16[4,256,256]{2,1,0:T(8,128)(2,1)S(1)} %shard_map.68.attended_ref, bf16[256,2048]{1,0:T(8,128)(2,1)S(1)} %get-tuple-element.23.hidden_ref, bf16[16,256,128]{2,1,0:T(8,128)(2,1)S(1)} %get-tuple-element.24.w0_ref, ...), custom_call_target="tpu_custom_call" | custom-call | tf_op jit(solution)/shard_map/pallas_call | solution.py:291
  (36 shorter events, 2.9 us)
Async XLA Ops:
  6.5 4.0 %copy-start = (bf16[48,1920]{1,0:T(8,128)(2,1)S(1)}, bf16[48,1920]{1,0:T(8,128)(2,1)}, u32[]{:S(2)}) copy-start(bf16[48,1920]{1,0:T(8,128)(2,1)} %param.7) | copy-start | bytes 552964
  6.5 106.1 %all-gather.3.cloned.1.call-start = ((), (), s32[]{:S(2)}) async-start(), calls=%async_computation.4 | async-start | bytes 4595712 | tf_op jit(solution)/shard_map/all_gather | solution.py:203
  83.8 7.3 %copy-start.2 = (bf16[1920]{0:T(1024)(128)(2,1)S(1)}, bf16[1920]{0:T(1024)(128)(2,1)}, u32[]{:S(2)}) copy-start(bf16[1920]{0:T(1024)(128)(2,1)} %param.10) | copy-start | bytes 11524
  85.0 18.4 %all-to-all-start.2 = ((bf16[32,48,256]{2,1,0:T(8,128)(2,1)}), bf16[32,48,256]{2,1,0:T(8,128)(2,1)S(1)}, u32[]{:S(2)}, u32[]{:S(2)}) async-start(bf16[32,48,256]{2,1,0:T(8,128)(2,1)} %bitcast.6), calls=%async_computation.2 | async-start | bytes 1572864 | tf_op jit(solution)/shard_map/all_to_all | solution.py:222
  112.6 2.2 %copy-start.1 = (bf16[2816,768]{1,0:T(8,128)(2,1)S(1)}, bf16[2816,768]{1,0:T(8,128)(2,1)}, u32[]{:S(2)}) copy-start(bf16[2816,768]{1,0:T(8,128)(2,1)} %all-gather.3.cloned.1.call-done) | copy-start | bytes 12976132
  114.8 46.0 %copy-start.3 = (s32[1,1,4]{2,1,0:T(1,128)S(1)}, s32[1,1,4]{2,1,0:T(1,128)}, u32[]{:S(2)}) copy-start(s32[1,1,4]{2,1,0:T(1,128)} %param.11) | copy-start | bytes 52
  117.1 27.3 %collective-permute-start.5 = (bf16[16,256,128]{2,1,0:T(8,128)(2,1)S(1)}, bf16[16,256,128]{2,1,0:T(8,128)(2,1)S(1)}, u32[]{:S(2)}, u32[]{:S(2)}) collective-permute-start(bf16[16,256,128]{2,1,0:T(8,128)(2,1)S(1)} %get-tuple-element.24.w0_ref), channel_id=1, source_target_pairs={{0,256},{128,384},{256,0},{384,128},{1,257},{129,385},{257,1},{385... | collective-permute-start | bytes 3145736 | tf_op jit(solution)/shard_map/ppermute | solution.py:247
  119.9 71.2 %collective-permute-start.4 = (bf16[16,256,128]{2,1,0:T(8,128)(2,1)S(1)}, bf16[16,256,128]{2,1,0:T(8,128)(2,1)}, u32[]{:S(2)}, u32[]{:S(2)}) collective-permute-start(bf16[16,256,128]{2,1,0:T(8,128)(2,1)S(1)} %get-tuple-element.24.w0_ref), channel_id=1, source_target_pairs={{0,128},{128,0},{256,384},{384,256},{1,129},{129,1},{257,385},{385... | collective-permute-start | bytes 3145736 | tf_op jit(solution)/shard_map/ppermute | solution.py:248
  144.4 46.7 %collective-permute-start.6 = (bf16[16,256,128]{2,1,0:T(8,128)(2,1)S(1)}, bf16[16,256,128]{2,1,0:T(8,128)(2,1)}, u32[]{:S(2)}, u32[]{:S(2)}) collective-permute-start(bf16[16,256,128]{2,1,0:T(8,128)(2,1)S(1)} %collective-permute-done.5.w2_ref), channel_id=1, source_target_pairs={{0,128},{128,0},{256,384},{384,256},{1,129},{129,1},{257,385},{385... | collective-permute-start | bytes 3145736 | tf_op jit(solution)/shard_map/ppermute | solution.py:249
  146.3 9.8 %all-to-all-start.3 = ((bf16[4,48,768]{2,1,0:T(8,128)(2,1)}), bf16[4,48,768]{2,1,0:T(8,128)(2,1)S(1)}, u32[]{:S(2)}, u32[]{:S(2)}) async-start(bf16[4,48,768]{2,1,0:T(8,128)(2,1)} %bitcast.11), calls=%async_computation.3 | async-start | bytes 589824 | tf_op jit(solution)/shard_map/all_to_all | solution.py:241
  149.7 9.8 %collective-permute-start.2 = (bf16[48,2048]{1,0:T(8,128)(2,1)}, bf16[48,2048]{1,0:T(8,128)(2,1)S(1)}, u32[]{:S(2)}, u32[]{:S(2)}) collective-permute-start(bf16[48,2048]{1,0:T(8,128)(2,1)} %get-tuple-element.17.own_ref), channel_id=1, source_target_pairs={{0,1},{1,2},{2,3},{3,4},{4,5},{5,6},{6,7},{7,8},{8,9},{9,10},{10,1... | collective-permute-start | bytes 589832 | tf_op jit(solution)/shard_map/ppermute | solution.py:233
  156.1 21.4 %collective-permute-start = (bf16[4,48,768]{2,1,0:T(8,128)(2,1)S(1)}, bf16[4,48,768]{2,1,0:T(8,128)(2,1)S(1)}, u32[]{:S(2)}, u32[]{:S(2)}) collective-permute-start(bf16[4,48,768]{2,1,0:T(8,128)(2,1)S(1)} %all-to-all-done.3.own_ref), channel_id=1, source_target_pairs={{0,1},{1,2},{2,3},{3,4},{4,5},{5,6},{6,7},{7,8},{8,9},{9,10},{10,1... | collective-permute-start | bytes 884744 | tf_op jit(solution)/shard_map/ppermute | solution.py:244
  158.2 19.2 %collective-permute-start.1 = (bf16[4,48,768]{2,1,0:T(8,128)(2,1)S(1)}, bf16[4,48,768]{2,1,0:T(8,128)(2,1)S(1)}, u32[]{:S(2)}, u32[]{:S(2)}) collective-permute-start(bf16[4,48,768]{2,1,0:T(8,128)(2,1)S(1)} %all-to-all-done.3.own_ref), channel_id=1, source_target_pairs={{1,0},{2,1},{3,2},{4,3},{5,4},{6,5},{7,6},{8,7},{9,8},{10,9},{11,1... | collective-permute-start | bytes 884744 | tf_op jit(solution)/shard_map/ppermute | solution.py:245
  159.5 14.0 %collective-permute-start.3 = (bf16[48,2048]{1,0:T(8,128)(2,1)}, bf16[48,2048]{1,0:T(8,128)(2,1)}, u32[]{:S(2)}, u32[]{:S(2)}) collective-permute-start(bf16[48,2048]{1,0:T(8,128)(2,1)} %get-tuple-element.17.own_ref), channel_id=1, source_target_pairs={{1,0},{2,1},{3,2},{4,3},{5,4},{6,5},{7,6},{8,7},{9,8},{10,9},{11,1... | collective-permute-start | bytes 589832 | tf_op jit(solution)/shard_map/ppermute | solution.py:234
Sparse Core Ops, SparseCore 0:
  9.5 102.4 all-gather.2

commit v2 on v1

--- a/solution.py
+++ b/solution.py
@@ -20,22 +20,59 @@
 BF16 = jnp.bfloat16
 
 
-def call(kernel, out_shape, vmem_mb, **kw):
+def call(kernel, out_shape, vmem_mb, mflops, kbytes, **kw):
     return pl.pallas_call(
         kernel,
         out_shape=out_shape,
         compiler_params=pltpu.CompilerParams(vmem_limit_bytes=vmem_mb << 20),
+        cost_estimate=pl.CostEstimate(flops=mflops * 10**6, bytes_accessed=kbytes * 1000, transcendentals=0),
         **kw,
     )
 
 
-def bridge_kernel(cells_ref, moved_ref, out_ref, weight_ref):
+def pack_kernel(place_ref, latent_ref, weight_ref, out_ref):
+    weight = weight_ref[...].astype(F32)
+    block = slice_of(weight, 0)
+    for ty in range(1, 8):
+        block = jnp.where(place_ref[0] == ty, slice_of(weight, ty), block)
+    chunks = [block[:, 0:LANES], block[:, LANES : 2 * LANES]]
+    latent = latent_ref[0].astype(F32)
     for t in range(16):
-        for b in range(3):
-            weight_ref[t * 48 + b * 16 : t * 48 + b * 16 + 16, :] = moved_ref[
-                t, 0:16, b * 256 : (b + 1) * 256
-            ]
-    sums = jnp.dot(cells_ref[...], weight_ref[...], preferred_element_type=F32).astype(BF16)
+        cells = jnp.concatenate([latent[0, 2 * t : 2 * t + 2], latent[1, 2 * t : 2 * t + 2]], axis=0)
+        cells = [cells[:, b * LANES : (b + 1) * LANES] for b in range(6)]
+        out_ref[t] = jnp.concatenate(chunks + cells, axis=0).astype(BF16)
+
+
+def slice_of(rows, ty):
+    lane = lax.broadcasted_iota(jnp.int32, (rows.shape[0], LANES), 1)
+    chunks = []
+    for t in (2 * ty, 2 * ty + 1):
+        tile, shift = divmod(t * CHUNK, LANES)
+        first = rows[:, tile * LANES : (tile + 1) * LANES]
+        if shift:
+            first = pltpu.roll(first, LANES - shift, 1)
+        if shift > LANES - CHUNK:
+            second = rows[:, (tile + 1) * LANES : (tile + 2) * LANES]
+            second = pltpu.roll(second, LANES - shift, 1)
+            first = jnp.where(lane < LANES - shift, first, second)
+        chunks.append(jnp.where(lane < CHUNK, first, 0.0))
+    return jnp.concatenate(chunks, axis=1)
+
+
+def spread_kernel(moved_ref, out_ref):
+    cells = moved_ref[:, 96:120, :].astype(F32)
+    cells = jnp.concatenate(
+        [cells[:, b * 4 : b * 4 + 4, :].reshape(64, LANES) for b in range(6)], axis=1
+    ).astype(BF16)
+    for ty in range(8):
+        out_ref[ty] = cells
+
+
+def bridge_kernel(cells_ref, moved_ref, out_ref):
+    weight = jnp.concatenate(
+        [moved_ref[:, c * 48 : c * 48 + 48, :].reshape(768, LANES) for c in range(2)], axis=1
+    )
+    sums = jnp.dot(cells_ref[...], weight, preferred_element_type=F32).astype(BF16)
     for y in range(8):
         for dy in range(3):
             source = min(max(y + dy - 1, 0), 7)
@@ -54,21 +91,50 @@
         gained_ref[:, lanes] = (total * gain_ref[:, lanes]).astype(BF16)
 
 
-def project_kernel(gained_ref, weights_ref, project_ref, out_weight_ref):
-    total = jnp.zeros(project_ref.shape, F32)
-    for t in range(CHUNKS):
+def project_kernel(gained_ref, weights_ref, project_ref, out_weight_ref, total_ref):
+    step = pl.program_id(0)
+    total = jnp.zeros(total_ref.shape, F32)
+    for t in range(4):
         total = total + jnp.dot(
-            gained_ref[:, t * LANES : (t + 1) * LANES],
-            weights_ref[t, 48:176, :],
+            gained_ref[:, t * LANES : t * LANES + CHUNK],
+            weights_ref[t, 48:168, :],
             preferred_element_type=F32,
         )
-    project_ref[...] = total.astype(BF16)
-    for t in range(CHUNKS):
         for b in range(6):
             rows = 48 if b < 5 else 16
             out_weight_ref[t, b * 48 : b * 48 + rows, :] = weights_ref[
                 t, 0:rows, b * LANES : (b + 1) * LANES
             ]
+
+    @pl.when(step == 0)
+    def _():
+        total_ref[...] = total
+
+    @pl.when(step > 0)
+    def _():
+        total_ref[...] += total
+
+    @pl.when(step == 3)
+    def _():
+        project_ref[...] = total_ref[...].astype(BF16)
+
+
+def tie_kernel(rows_ref, after_ref, out_ref):
+    pass
+
+
+def tie(rows, after):
+    anywhere = pl.BlockSpec(memory_space=pl.ANY)
+    return call(
+        tie_kernel,
+        jax.ShapeDtypeStruct(rows.shape, rows.dtype),
+        4,
+        1,
+        1,
+        in_specs=[anywhere, anywhere],
+        out_specs=anywhere,
+        input_output_aliases={0: 0},
+    )(rows, after)
 
 
 def axis_weight(fine, cell, low, high):
@@ -130,7 +196,8 @@
         & (col >= -place_ref[4])
         & (col < 8 + place_ref[5])
     )
-    bias_ref[...] = jnp.where(allowed, 0.0, NEG)
+    lane = lax.broadcasted_iota(jnp.int32, (1024, LANES), 1)
+    bias_ref[...] = jnp.where(((lane & (HD - 1)) == 0) & ~allowed, NEG, 0.0)
 
 
 def attend_kernel(
@@ -145,9 +212,9 @@
     third = fine[:, 256:384] * scale
     lane = lax.broadcasted_iota(jnp.int32, (1024, LANES), 1)
     low = lane < HD
-    key_0 = jnp.where(low, jnp.where(lane == 0, bias, 0.0), first).astype(BF16)
+    key_0 = jnp.where(low, bias, first).astype(BF16)
     value_0 = jnp.where(low, second, 1.0).astype(BF16)
-    key_1 = jnp.where(low, third, jnp.where(lane == HD, bias, 0.0)).astype(BF16)
+    key_1 = jnp.where(low, third, bias).astype(BF16)
     value_1 = jnp.where(low, 1.0, third).astype(BF16)
     query = jnp.dot(query_ref[...], patch[:, 0:256], preferred_element_type=F32)
     query_scale = query_scale_ref[...] * (HD ** (-0.5) * 1.4426950408889634)
@@ -169,16 +236,27 @@
     out_ref[0] = mixed.astype(BF16)
 
 
-def output_kernel(place_ref, attended_ref, hidden_ref, w0_ref, w1_ref, w2_ref, w3_ref, out_ref):
+def times_rows(group, rows, t):
+    pair = jnp.concatenate([rows[t], rows[t + 1]], axis=1)
+    return jnp.dot(group, pair, preferred_element_type=F32)
+
+
+def partial_kernel(place_ref, attended_ref, hidden_ref, own_ref, near_ref, far_ref, out_ref):
     rep = place_ref[0]
-    weights = (w0_ref, w1_ref, w2_ref, w3_ref)
-    groups = [attended_ref[rep ^ k] for k in range(4)]
+    groups = [attended_ref[rep ^ k] for k in range(3)]
+    for t in range(0, CHUNKS, 2):
+        lanes = slice(t * LANES, (t + 2) * LANES)
+        total = hidden_ref[:, lanes].astype(F32)
+        for group, rows in zip(groups, (own_ref, near_ref, far_ref)):
+            total = total + times_rows(group, rows, t)
+        out_ref[:, lanes] = total
+
+
+def output_kernel(place_ref, attended_ref, total_ref, last_ref, out_ref):
+    group = attended_ref[place_ref[0] ^ 3]
     chunks = []
     for t in range(0, CHUNKS, 2):
-        total = hidden_ref[:, t * LANES : (t + 2) * LANES].astype(F32)
-        for k in range(4):
-            pair = jnp.concatenate([weights[k][t], weights[k][t + 1]], axis=1)
-            total = total + jnp.dot(groups[k], pair, preferred_element_type=F32)
+        total = total_ref[:, t * LANES : (t + 2) * LANES] + times_rows(group, last_ref, t)
         chunks.append(total[:, 0:LANES])
         chunks.append(total[:, LANES : 2 * LANES])
     lane = lax.broadcasted_iota(jnp.int32, (256, LANES), 1)
@@ -197,34 +275,31 @@
     smem = pl.BlockSpec(memory_space=pltpu.SMEM)
 
     out_rows = jnp.pad(out_weight, ((0, 32), (0, LANES - CHUNK))).reshape(6, 48, LANES)
-    shard = jnp.concatenate(
-        [out_rows.transpose(1, 0, 2).reshape(48, 768), qkv_weight, jnp.zeros((8, 768), BF16)], axis=0
-    )
+    shard = jnp.concatenate([out_rows.transpose(1, 0, 2).reshape(48, 768), qkv_weight], axis=0)
     gathered = lax.all_gather(shard, "tx", axis=0)
 
-    source = lax.broadcasted_iota(jnp.int32, (WIDTH, 256), 0)
-    target = lax.broadcasted_iota(jnp.int32, (WIDTH, 256), 1)
-    inside = target & 127
-    pick = ((inside < CHUNK) & (source == ty * 240 + (target >> 7) * CHUNK + inside)).astype(BF16)
-    columns = jnp.dot(in_weight, pick, preferred_element_type=F32).astype(BF16)
-    columns = columns.reshape(3, 16, 256).transpose(1, 0, 2).reshape(1, 16, 768)
-    tiles = latent.reshape(2, 16, 2, 768).transpose(1, 0, 2, 3).reshape(16, 4, 768)
-    message = jnp.concatenate([jnp.broadcast_to(columns, (16, 16, 768)), tiles], axis=1)
+    vmem = pl.BlockSpec(memory_space=pltpu.VMEM)
+    message = call(
+        pack_kernel,
+        jax.ShapeDtypeStruct((16, 120, LANES), BF16),
+        16,
+        10,
+        500,
+        in_specs=[smem, vmem, vmem],
+        out_specs=vmem,
+    )(ty.astype(jnp.int32).reshape(1), latent, in_weight)
     moved = lax.all_to_all(message, "tx", split_axis=0, concat_axis=0, tiled=True)
-    cells = moved[:, 16:20, :].reshape(1, 64, 768)
-    cells = lax.all_to_all(jnp.broadcast_to(cells, (8, 64, 768)), "ty", split_axis=0, concat_axis=0, tiled=True)
-    sums = call(
-        bridge_kernel,
-        jax.ShapeDtypeStruct((4, 8, 3, 16, 256), BF16),
-        16,
-        scratch_shapes=[pltpu.VMEM((768, 256), BF16)],
-    )(cells.reshape(512, 768), moved)
+    cells = call(spread_kernel, jax.ShapeDtypeStruct((8, 64, 768), BF16), 16, 10, 1500)(moved)
+    cells = lax.all_to_all(cells, "ty", split_axis=0, concat_axis=0, tiled=True)
+    sums = call(bridge_kernel, jax.ShapeDtypeStruct((4, 8, 3, 16, 256), BF16), 16, 800, 2000)(
+        cells.reshape(512, 768), moved
+    )
     parts = lax.all_to_all(
         sums.reshape(32, CELLS, 256), ("rep", "ty"), split_axis=0, concat_axis=0, tiled=True
     )
     gain = jnp.pad(norm_gain.astype(F32).reshape(CHUNKS, CHUNK), ((0, 0), (0, LANES - CHUNK))).reshape(1, WIDE)
     coarse, gained = call(
-        reduce_kernel, [jax.ShapeDtypeStruct((CELLS, WIDE), BF16)] * 2, 16
+        reduce_kernel, [jax.ShapeDtypeStruct((CELLS, WIDE), BF16)] * 2, 16, 100, 2000
     )(parts, gain)
 
     count = lax.axis_size("tx")
@@ -237,19 +312,30 @@
         project_kernel,
         [jax.ShapeDtypeStruct((4 * CELLS, 768), BF16), jax.ShapeDtypeStruct((CHUNKS, 256, LANES), BF16)],
         32,
+        1000,
+        6000,
+        grid=(4,),
+        in_specs=[
+            pl.BlockSpec((4 * CELLS, 4 * LANES), lambda k: (0, k)),
+            pl.BlockSpec((4, 168, 768), lambda k: (k, 0, 0)),
+        ],
+        out_specs=[
+            pl.BlockSpec((4 * CELLS, 768), lambda k: (0, 0)),
+            pl.BlockSpec((4, 256, LANES), lambda k: (k, 0, 0)),
+        ],
+        scratch_shapes=[pltpu.VMEM((4 * CELLS, 768), F32)],
     )(gained, gathered)
     project = lax.all_to_all(
         project.reshape(4, CELLS, 768), "rep", split_axis=0, concat_axis=0, tiled=True
     )
+    own_rows = tie(own_rows, project)
     project_left = lax.ppermute(project, "tx", to_right)
     project_right = lax.ppermute(project, "tx", to_left)
 
     far_rows = lax.ppermute(own_rows, "rep", [(i, i ^ 2) for i in range(4)])
     near_rows = lax.ppermute(own_rows, "rep", [(i, i ^ 1) for i in range(4)])
-    last_rows = lax.ppermute(far_rows, "rep", [(i, i ^ 1) for i in range(4)])
 
     place = jnp.concatenate([jnp.stack([ty, tx]).astype(jnp.int32), extents.reshape(4)])
-    vmem = pl.BlockSpec(memory_space=pltpu.VMEM)
     keys, query, key_scale, query_scale, bias, hidden = call(
         norm_kernel,
         [
@@ -261,19 +347,22 @@
             jax.ShapeDtypeStruct((256, WIDE), BF16),
         ],
         32,
+        2000,
+        8000,
         in_specs=[smem, vmem, vmem, vmem],
         out_specs=[vmem] * 6,
     )(place, coarse_left, coarse, coarse_right)
 
-    piece = pl.BlockSpec((1, CELLS, 384), lambda p: (p // 2, 0, p % 2))
-
     def whole(shape):
         return pl.BlockSpec(shape, lambda p: (0, 0))
 
+    piece = pl.BlockSpec((1, CELLS, 384), lambda p: (p // 2, 0, p % 2))
     attended = call(
         attend_kernel,
         jax.ShapeDtypeStruct((4, 256, 256), BF16),
         32,
+        10000,
+        40000,
         grid=(8,),
         in_specs=[
             piece,
@@ -288,13 +377,27 @@
         out_specs=pl.BlockSpec((1, 256, LANES), lambda p: (p // 2, 0, p % 2)),
     )(project_left, project, project_right, keys, query, key_scale, query_scale, bias)
 
+    far_rows = tie(far_rows, attended)
+    last_rows = lax.ppermute(far_rows, "rep", [(i, i ^ 1) for i in range(4)])
+    group = rep.astype(jnp.int32).reshape(1)
+    total = call(
+        partial_kernel,
+        jax.ShapeDtypeStruct((256, WIDE), F32),
+        32,
+        1000,
+        6000,
+        in_specs=[smem] + [vmem] * 5,
+        out_specs=vmem,
+    )(group, attended, hidden, own_rows, near_rows, far_rows)
     result = call(
         output_kernel,
         jax.ShapeDtypeStruct((256, WIDTH), BF16),
         32,
-        in_specs=[smem] + [vmem] * 6,
+        300,
+        3000,
+        in_specs=[smem] + [vmem] * 3,
         out_specs=vmem,
-    )(rep.astype(jnp.int32).reshape(1), attended, hidden, own_rows, near_rows, far_rows, last_rows)
+    )(group, attended, total, last_rows)
     return result.reshape(4, 8, 8, WIDTH)
 
 

time: 204 us -> 171 us (0.84)
  waiting for transfers between devices: 51.6 us -> 21.8 us
  blocking collectives: 80.9 us -> 71.6 us
  starting transfers between devices: 23 us -> 25.9 us
  local copies, waits for them, and re-layouts: 4.63 us -> 7.26 us
    ppermute x1, waiting for transfers between devices: 22.5 us -> 2.76 us  [body(): far_rows = lax.ppermute(own_rows, 'rep', [(i, i ^ 2) for i in range(4)])]
    ppermute x1, waiting for transfers between devices: 12.6 us -> 0.01 us  [body(): coarse_right = lax.ppermute(coarse, 'tx', to_left)]
    all_to_all x1, blocking collectives: 56.4 us -> 47 us  [body(): lax.all_to_all(message, 'tx', split_axis=0, concat_axis=0, tiled=True)]
    all_gather x1, waiting for transfers between devices: 0.01 us -> 4.99 us  [body(): gathered = lax.all_gather(shard, 'tx', axis=0)]
    unnamed x10 -> x15, local copies, waits for them, and re-layouts: 3.22 us -> 7.13 us
    all_to_all x1, waiting for transfers between devices: 4.21 us -> 1.77 us  [body(): lax.all_to_all(project.reshape(4, CELLS, 768), 'rep', split_axis=0, conca...]
    pallas_call x4 -> x9, Pallas kernels: 19.5 us -> 20.1 us  [the longest x1 13.5 us: body(): call(attend_kernel, jax.ShapeDtypeStruct((4, 256, 256), BF16), 32, 10000,...]
  transfers between devices with their start and end apart: 10 -> 10, of which waited for: 4 -> 4; matrix products, arithmetic and copies ran while one was open for 1% -> 0% of each run, Pallas kernels for 10% -> 12%
where the time goes in v2:
time: 171 us; the launch traced here: 169 us
  blocking collectives  71.6 us (42%)
  Pallas kernels  26.8 us (16%)
  starting transfers between devices  25.9 us (15%)
  waiting for transfers between devices  21.8 us (13%)
  between operations  13.7 us (8%)
  local copies, waits for them, and re-layouts  7.26 us (4%)
  other arithmetic  1.72 us (1%)
    all_to_all x1, blocking collectives, body(): lax.all_to_all(message, 'tx', split_axis=0, concat_axis=0, tiled=True)  47 us
    all_to_all x1, blocking collectives, body(): cells = lax.all_to_all(cells, 'ty', split_axis=0, concat_axis=0, tiled=True)  16.1 us
    pallas_call x1, Pallas kernels, body(): call(attend_kernel, jax.ShapeDtypeStruct((4, 256, 256), BF16), 32, 10000,...  13.5 us
    all_to_all x1, waiting for transfers between devices, body(): lax.all_to_all(sums.reshape(32, CELLS, 256), ('rep', 'ty'), split_axis=0,...  12.2 us
    all_gather x1, blocking collectives, body(): gained = lax.all_gather(gained, 'rep', axis=0, tiled=True)  8.51 us
    unnamed x15, local copies, waits for them, and re-layouts  7.13 us
    all_to_all x1, starting transfers between devices, body(): lax.all_to_all(sums.reshape(32, CELLS, 256), ('rep', 'ty'), split_axis=0,...  6.13 us
    all_gather x1, waiting for transfers between devices, body(): gathered = lax.all_gather(shard, 'tx', axis=0)  4.99 us
  transfers between devices with their start and end apart: 10, of which 4 were waited for; matrix products, arithmetic and copies ran while one was open for 0% of the time, Pallas kernels for 12%

profile of v2, /device:TPU:24, one launch (start us, length us, event | category | flops | bytes accessed | tf_op | source)
XLA Modules:
  0.0 168.8 jit_solution(15076666888429848367)
XLA Ops:
  7.5 1.6 pad_maximum_fusion
  11.3 47.0 %all_to_all.20.moved_ref = bf16[16,120,128]{2,1,0:T(8,128)(2,1)S(1)} all-to-all(bf16[16,120,128]{2,1,0:T(8,128)(2,1)S(1)} %shard_map.64), channel_id=1, replica_groups=mesh['rep'=4,'ty'=8,'tx'=16] {'tx'}, dimensions={0} | all-to-all | bytes 983040 | tf_op jit(solution)/shard_map/all_to_all | solution.py:291
  58.3 16.1 %all_to_all.21 = bf16[8,64,768]{2,1,0:T(8,128)(2,1)S(1)} all-to-all(bf16[8,64,768]{2,1,0:T(8,128)(2,1)S(1)} %shard_map.65), channel_id=1, replica_groups=mesh['rep'=4,'ty'=8,'tx'=16] {'ty'}, dimensions={0} | all-to-all | bytes 1572864 | tf_op jit(solution)/shard_map/all_to_all | solution.py:293
  74.4 1.3 shard_map.66
  75.7 6.1 %all-to-all-start.2 = ((bf16[32,48,256]{2,1,0:T(8,128)(2,1)}), bf16[32,48,256]{2,1,0:T(8,128)(2,1)S(1)}, u32[]{:S(2)}, u32[]{:S(2)}) async-start(bf16[32,48,256]{2,1,0:T(8,128)(2,1)} %bitcast.3), calls=%async_computation.2 | async-start | bytes 1572864 | tf_op jit(solution)/shard_map/all_to_all | solution.py:297
  81.9 12.2 %all-to-all-done.2.parts_ref = bf16[32,48,256]{2,1,0:T(8,128)(2,1)S(1)} async-done(((bf16[32,48,256]{2,1,0:T(8,128)(2,1)}), bf16[32,48,256]{2,1,0:T(8,128)(2,1)S(1)}, u32[]{:S(2)}, u32[]{:S(2)}) %all-to-all-start.2) | async-done | bytes 786464 | tf_op jit(solution)/shard_map/all_to_all | solution.py:297
  94.3 8.5 %all_gather.9.gained_ref = bf16[192,2048]{1,0:T(8,128)(2,1)S(1)} all-gather(bf16[48,2048]{1,0:T(8,128)(2,1)S(1)} %get-tuple-element.15), channel_id=1, replica_groups=mesh['rep'=4,'ty'=8,'tx'=16] {'rep'}, dimensions={0}, use_global_device_ids=true | all-gather | bytes 983040 | tf_op jit(solution)/shard_map/all_gather | solution.py:310
  102.8 5.0 %all-gather.3.cloned.1.call-done = bf16[2688,768]{1,0:T(8,128)(2,1)} async-done(((bf16[168,768]{1,0:T(8,128)(2,1)}), bf16[2688,768]{1,0:T(8,128)(2,1)}) %all-gather.3.cloned.1.call-update) | async-done | bytes 4128784 | tf_op jit(solution)/shard_map/all_gather | solution.py:279
  107.8 2.2 %copy-done = bf16[2688,768]{1,0:T(8,128)(2,1)S(1)} copy-done((bf16[2688,768]{1,0:T(8,128)(2,1)S(1)}, bf16[2688,768]{1,0:T(8,128)(2,1)}, u32[]{:S(2)}) %copy-start) | copy-done | bytes 4128792
  109.9 3.1 %shard_map.68 = (bf16[192,768]{1,0:T(8,128)(2,1)}, bf16[16,256,128]{2,1,0:T(8,128)(2,1)S(1)}) custom-call(bf16[192,2048]{1,0:T(8,128)(2,1)S(1)} %all_gather.9.gained_ref, bf16[16,168,768]{2,1,0:T(8,128)(2,1)S(1)} %bitcast.17), custom_call_target="tpu_custom_call" | custom-call | flops 1000000000 | bytes 6000000 | tf_op jit(solution)/shard_map/pallas_call | solution.py:311
  113.0 3.5 %all-to-all-start.3 = ((bf16[4,48,768]{2,1,0:T(8,128)(2,1)}), bf16[4,48,768]{2,1,0:T(8,128)(2,1)S(1)}, u32[]{:S(2)}, u32[]{:S(2)}) async-start(bf16[4,48,768]{2,1,0:T(8,128)(2,1)} %bitcast.8), calls=%async_computation.3 | async-start | bytes 589824 | tf_op jit(solution)/shard_map/all_to_all | solution.py:328
  116.5 3.3 %collective-permute-start.2 = (bf16[48,2048]{1,0:T(8,128)(2,1)S(1)}, bf16[48,2048]{1,0:T(8,128)(2,1)S(1)}, u32[]{:S(2)}, u32[]{:S(2)}) collective-permute-start(bf16[48,2048]{1,0:T(8,128)(2,1)S(1)} %get-tuple-element.17.own_ref), channel_id=1, source_target_pairs={{0,1},{1,2},{2,3},{3,4},{4,5},{5,6},{6,7},{7,8},{8,9},{9,10},{10,1... | collective-permute-start | bytes 589832 | tf_op jit(solution)/shard_map/ppermute | solution.py:308
  119.7 1.3 collective-permute-start.3
  121.0 1.8 %all-to-all-done.3.own_ref.after_ref = bf16[4,48,768]{2,1,0:T(8,128)(2,1)S(1)} async-done(((bf16[4,48,768]{2,1,0:T(8,128)(2,1)}), bf16[4,48,768]{2,1,0:T(8,128)(2,1)S(1)}, u32[]{:S(2)}, u32[]{:S(2)}) %all-to-all-start.3) | async-done | bytes 294944 | tf_op jit(solution)/shard_map/all_to_all | solution.py:328
  122.8 3.3 %collective-permute-start = (bf16[4,48,768]{2,1,0:T(8,128)(2,1)S(1)}, bf16[4,48,768]{2,1,0:T(8,128)(2,1)S(1)}, u32[]{:S(2)}, u32[]{:S(2)}) collective-permute-start(bf16[4,48,768]{2,1,0:T(8,128)(2,1)S(1)} %all-to-all-done.3.own_ref.after_ref), channel_id=1, source_target_pairs={{0,1},{1,2},{2,3},{3,4},{4,5},{5,6},{6,7},{7,8},{8,9},{9,10},{10,1... | collective-permute-start | bytes 884744 | tf_op jit(solution)/shard_map/ppermute | solution.py:332
  126.1 1.3 collective-permute-start.1
  127.5 3.4 %collective-permute-start.5 = (bf16[16,256,128]{2,1,0:T(8,128)(2,1)S(1)}, bf16[16,256,128]{2,1,0:T(8,128)(2,1)S(1)}, u32[]{:S(2)}, u32[]{:S(2)}) collective-permute-start(bf16[16,256,128]{2,1,0:T(8,128)(2,1)S(1)} %shard_map.71.own_ref), channel_id=1, source_target_pairs={{0,256},{128,384},{256,0},{384,128},{1,257},{129,385},{257,1},{385... | collective-permute-start | bytes 3145736 | tf_op jit(solution)/shard_map/ppermute | solution.py:335
  130.9 3.6 %shard_map.69 = (bf16[1024,144]{1,0:T(8,128)(2,1)S(1)}, bf16[256,144]{1,0:T(8,128)(2,1)S(1)}, f32[1024,128]{1,0:T(8,128)S(1)}, f32[256,128]{1,0:T(8,128)S(1)}, f...) custom-call(s32[6]{0:T(128)S(1)} %pad_add_fusion.place_ref, bf16[48,2048]{1,0:T(8,128)(2,1)S(1)} %collective-permute-done.2.left_ref, ...), custom_call_target="tpu_custom_call" | custom-call | flops 2000000000 | bytes 8000000 | tf_op jit(solution)/shard_map/pallas_call | solution.py:339
  135.6 1.9 %collective-permute-start.4 = (bf16[16,256,128]{2,1,0:T(8,128)(2,1)S(1)}, bf16[16,256,128]{2,1,0:T(8,128)(2,1)}, u32[]{:S(2)}, u32[]{:S(2)}) collective-permute-start(bf16[16,256,128]{2,1,0:T(8,128)(2,1)S(1)} %shard_map.71.own_ref), channel_id=1, source_target_pairs={{0,128},{128,0},{256,384},{384,256},{1,129},{129,1},{257,385},{385... | collective-permute-start | bytes 3145736 | tf_op jit(solution)/shard_map/ppermute | solution.py:336
  137.5 13.5 %shard_map.70.after_ref.attended_ref = bf16[4,256,256]{2,1,0:T(8,128)(2,1)S(1)} custom-call(bf16[4,48,768]{2,1,0:T(8,128)(2,1)S(1)} %collective-permute-done.left_ref, bf16[4,48,768]{2,1,0:T(8,128)(2,1)S(1)} %all-to-all-done.3.own_ref.after_ref, bf16[4,48,768]{2,1,0:T(8,128)(2,1)S(1)} %collective-permute-done.1.right_ref, ...), custom_call_target="tpu_custom_call" | custom-call | flops 10000000000 | bytes 40000000 | tf_op jit(solution)/shard_map/pallas_call | solution.py:360
  151.0 2.8 %collective-permute-done.5.rows_ref = bf16[16,256,128]{2,1,0:T(8,128)(2,1)S(1)} collective-permute-done((bf16[16,256,128]{2,1,0:T(8,128)(2,1)S(1)}, bf16[16,256,128]{2,1,0:T(8,128)(2,1)S(1)}, u32[]{:S(2)}, u32[]{:S(2)}) %collective-permute-start.5) | collective-permute-done | bytes 1048608 | tf_op jit(solution)/shard_map/ppermute | solution.py:335
  153.8 1.9 %collective-permute-start.6 = (bf16[16,256,128]{2,1,0:T(8,128)(2,1)S(1)}, bf16[16,256,128]{2,1,0:T(8,128)(2,1)}, u32[]{:S(2)}, u32[]{:S(2)}) collective-permute-start(bf16[16,256,128]{2,1,0:T(8,128)(2,1)S(1)} %shard_map.72.far_ref), channel_id=1, source_target_pairs={{0,128},{128,0},{256,384},{384,256},{1,129},{129,1},{257,385},{385... | collective-permute-start | bytes 3145736 | tf_op jit(solution)/shard_map/ppermute | solution.py:381
  156.9 2.2 %shard_map.73.total_ref = f32[256,2048]{1,0:T(8,128)S(1)} custom-call(s32[1]{0:T(128)} %bitcast.place_ref, bf16[4,256,256]{2,1,0:T(8,128)(2,1)S(1)} %shard_map.70.after_ref.attended_ref, bf16[256,2048]{1,0:T(8,128)(2,1)S(1)} %copy-done.2, bf16[16,256,128]{2,1,0:T(8,128)(2,1)S(1)} %shard_map.71.own_ref, ...), custom_call_target="tpu_custom_call" | custom-call | flops 1000000000 | bytes 6000000 | tf_op jit(solution)/shard_map/pallas_call | solution.py:383
  159.2 2.7 %shard_map.74 = bf16[256,1920]{1,0:T(8,128)(2,1)} custom-call(s32[1]{0:T(128)} %bitcast.place_ref, bf16[4,256,256]{2,1,0:T(8,128)(2,1)S(1)} %shard_map.70.after_ref.attended_ref, f32[256,2048]{1,0:T(8,128)S(1)} %shard_map.73.total_ref, bf16[16,256,128]{2,1,0:T(8,128)(2,1)} %collective-permute-done.6.last_ref), custom_call_target="tpu_custom_call" | custom-call | flops 300000000 | bytes 3000000 | tf_op jit(solution)/shard_map/pallas_call | solution.py:392
  (32 shorter events, 5.6 us)
Async XLA Ops:
  6.5 101.2 %all-gather.3.cloned.1.call-start = ((), (), s32[]{:S(2)}) async-start(), calls=%async_computation.4 | async-start | bytes 4386816 | tf_op jit(solution)/shard_map/all_gather | solution.py:279
  9.2 0.9 copy-start.3
  10.1 0.9 copy-start.4
  11.2 70.6 %copy-start.5 = (bf16[1920]{0:T(1024)(128)(2,1)S(1)}, bf16[1920]{0:T(1024)(128)(2,1)}, u32[]{:S(2)}) copy-start(bf16[1920]{0:T(1024)(128)(2,1)} %param.10) | copy-start | bytes 11524
  75.7 51.7 %copy-start.6 = (s32[1,1,4]{2,1,0:T(1,128)S(1)}, s32[1,1,4]{2,1,0:T(1,128)}, u32[]{:S(2)}) copy-start(s32[1,1,4]{2,1,0:T(1,128)} %param.11) | copy-start | bytes 52
  75.7 18.5 %all-to-all-start.2 = ((bf16[32,48,256]{2,1,0:T(8,128)(2,1)}), bf16[32,48,256]{2,1,0:T(8,128)(2,1)S(1)}, u32[]{:S(2)}, u32[]{:S(2)}) async-start(bf16[32,48,256]{2,1,0:T(8,128)(2,1)} %bitcast.3), calls=%async_computation.2 | async-start | bytes 1572864 | tf_op jit(solution)/shard_map/all_to_all | solution.py:297
  107.8 2.2 %copy-start = (bf16[2688,768]{1,0:T(8,128)(2,1)S(1)}, bf16[2688,768]{1,0:T(8,128)(2,1)}, u32[]{:S(2)}) copy-start(bf16[2688,768]{1,0:T(8,128)(2,1)} %all-gather.3.cloned.1.call-done) | copy-start | bytes 12386308
  113.0 9.8 %all-to-all-start.3 = ((bf16[4,48,768]{2,1,0:T(8,128)(2,1)}), bf16[4,48,768]{2,1,0:T(8,128)(2,1)S(1)}, u32[]{:S(2)}, u32[]{:S(2)}) async-start(bf16[4,48,768]{2,1,0:T(8,128)(2,1)} %bitcast.8), calls=%async_computation.3 | async-start | bytes 589824 | tf_op jit(solution)/shard_map/all_to_all | solution.py:328
  116.5 14.4 %collective-permute-start.2 = (bf16[48,2048]{1,0:T(8,128)(2,1)S(1)}, bf16[48,2048]{1,0:T(8,128)(2,1)S(1)}, u32[]{:S(2)}, u32[]{:S(2)}) collective-permute-start(bf16[48,2048]{1,0:T(8,128)(2,1)S(1)} %get-tuple-element.17.own_ref), channel_id=1, source_target_pairs={{0,1},{1,2},{2,3},{3,4},{4,5},{5,6},{6,7},{7,8},{8,9},{9,10},{10,1... | collective-permute-start | bytes 589832 | tf_op jit(solution)/shard_map/ppermute | solution.py:308
  119.7 11.2 %collective-permute-start.3 = (bf16[48,2048]{1,0:T(8,128)(2,1)S(1)}, bf16[48,2048]{1,0:T(8,128)(2,1)S(1)}, u32[]{:S(2)}, u32[]{:S(2)}) collective-permute-start(bf16[48,2048]{1,0:T(8,128)(2,1)S(1)} %get-tuple-element.17.own_ref), channel_id=1, source_target_pairs={{1,0},{2,1},{3,2},{4,3},{5,4},{6,5},{7,6},{8,7},{9,8},{10,9},{11,1... | collective-permute-start | bytes 589832 | tf_op jit(solution)/shard_map/ppermute | solution.py:309
  122.8 14.7 %collective-permute-start = (bf16[4,48,768]{2,1,0:T(8,128)(2,1)S(1)}, bf16[4,48,768]{2,1,0:T(8,128)(2,1)S(1)}, u32[]{:S(2)}, u32[]{:S(2)}) collective-permute-start(bf16[4,48,768]{2,1,0:T(8,128)(2,1)S(1)} %all-to-all-done.3.own_ref.after_ref), channel_id=1, source_target_pairs={{0,1},{1,2},{2,3},{3,4},{4,5},{5,6},{6,7},{7,8},{8,9},{9,10},{10,1... | collective-permute-start | bytes 884744 | tf_op jit(solution)/shard_map/ppermute | solution.py:332
  126.1 11.4 %collective-permute-start.1 = (bf16[4,48,768]{2,1,0:T(8,128)(2,1)S(1)}, bf16[4,48,768]{2,1,0:T(8,128)(2,1)S(1)}, u32[]{:S(2)}, u32[]{:S(2)}) collective-permute-start(bf16[4,48,768]{2,1,0:T(8,128)(2,1)S(1)} %all-to-all-done.3.own_ref.after_ref), channel_id=1, source_target_pairs={{1,0},{2,1},{3,2},{4,3},{5,4},{6,5},{7,6},{8,7},{9,8},{10,9},{11,1... | collective-permute-start | bytes 884744 | tf_op jit(solution)/shard_map/ppermute | solution.py:333
  127.5 26.3 %collective-permute-start.5 = (bf16[16,256,128]{2,1,0:T(8,128)(2,1)S(1)}, bf16[16,256,128]{2,1,0:T(8,128)(2,1)S(1)}, u32[]{:S(2)}, u32[]{:S(2)}) collective-permute-start(bf16[16,256,128]{2,1,0:T(8,128)(2,1)S(1)} %shard_map.71.own_ref), channel_id=1, source_target_pairs={{0,256},{128,384},{256,0},{384,128},{1,257},{129,385},{257,1},{385... | collective-permute-start | bytes 3145736 | tf_op jit(solution)/shard_map/ppermute | solution.py:335
  134.6 1.0 copy-start.1
  135.6 20.1 %collective-permute-start.4 = (bf16[16,256,128]{2,1,0:T(8,128)(2,1)S(1)}, bf16[16,256,128]{2,1,0:T(8,128)(2,1)}, u32[]{:S(2)}, u32[]{:S(2)}) collective-permute-start(bf16[16,256,128]{2,1,0:T(8,128)(2,1)S(1)} %shard_map.71.own_ref), channel_id=1, source_target_pairs={{0,128},{128,0},{256,384},{384,256},{1,129},{129,1},{257,385},{385... | collective-permute-start | bytes 3145736 | tf_op jit(solution)/shard_map/ppermute | solution.py:336
  153.8 5.4 %collective-permute-start.6 = (bf16[16,256,128]{2,1,0:T(8,128)(2,1)S(1)}, bf16[16,256,128]{2,1,0:T(8,128)(2,1)}, u32[]{:S(2)}, u32[]{:S(2)}) collective-permute-start(bf16[16,256,128]{2,1,0:T(8,128)(2,1)S(1)} %shard_map.72.far_ref), channel_id=1, source_target_pairs={{0,128},{128,0},{256,384},{384,256},{1,129},{129,1},{257,385},{385... | collective-permute-start | bytes 3145736 | tf_op jit(solution)/shard_map/ppermute | solution.py:381
  155.7 1.2 copy-start.2
Sparse Core Ops, SparseCore 0:
  9.4 98.2 all-gather.2

commit v3 on v1

--- a/solution.py
+++ b/solution.py
@@ -20,22 +20,84 @@
 BF16 = jnp.bfloat16
 
 
-def call(kernel, out_shape, vmem_mb, **kw):
+def call(kernel, out_shape, vmem_mb, mflops, kbytes, **kw):
     return pl.pallas_call(
         kernel,
         out_shape=out_shape,
         compiler_params=pltpu.CompilerParams(vmem_limit_bytes=vmem_mb << 20),
+        cost_estimate=pl.CostEstimate(flops=mflops * 10**6, bytes_accessed=kbytes * 1000, transcendentals=0),
         **kw,
     )
 
 
-def bridge_kernel(cells_ref, moved_ref, out_ref, weight_ref):
+def start_kernel(
+    place_ref, latent_hbm, weight_hbm, qkv_hbm, out_weight_hbm, message_ref, shard_ref, latent_ref, weight_ref, qkv_ref, out_weight_ref, sems
+):
+    copies = [
+        pltpu.make_async_copy(source, target, sems.at[i])
+        for i, (source, target) in enumerate(
+            (
+                (out_weight_hbm, out_weight_ref),
+                (qkv_hbm, qkv_ref),
+                (weight_hbm, weight_ref),
+                (latent_hbm, latent_ref),
+            )
+        )
+    ]
+    for copy in copies:
+        copy.start()
+    copies[0].wait()
+    rows = out_weight_ref[...].astype(F32)
+    rows = jnp.concatenate([rows, jnp.zeros((LANES - CHUNK, 256), F32)], axis=0).T
+    rows = jnp.concatenate([rows, jnp.zeros((32, LANES), F32)], axis=0)
+    rows = jnp.concatenate([rows[b * 48 : (b + 1) * 48] for b in range(6)], axis=1)
+    shard_ref[128:176, :] = rows.astype(BF16)
+    copies[1].wait()
+    shard_ref[0:128, :] = jnp.concatenate([qkv_ref[...], jnp.zeros((8, 768), BF16)], axis=0)
+    copies[2].wait()
+    weight = weight_ref[...].astype(F32)
+    block = slice_of(weight, 0)
+    for ty in range(1, 8):
+        block = jnp.where(place_ref[0] == ty, slice_of(weight, ty), block)
+    chunks = [block[:, 0:LANES], block[:, LANES : 2 * LANES]]
+    copies[3].wait()
+    latent = latent_ref[0].astype(F32)
     for t in range(16):
-        for b in range(3):
-            weight_ref[t * 48 + b * 16 : t * 48 + b * 16 + 16, :] = moved_ref[
-                t, 0:16, b * 256 : (b + 1) * 256
-            ]
-    sums = jnp.dot(cells_ref[...], weight_ref[...], preferred_element_type=F32).astype(BF16)
+        cells = jnp.concatenate([latent[0, 2 * t : 2 * t + 2], latent[1, 2 * t : 2 * t + 2]], axis=0)
+        cells = [cells[:, b * LANES : (b + 1) * LANES] for b in range(6)]
+        message_ref[t] = jnp.concatenate(chunks + cells, axis=0).astype(BF16)
+
+
+def slice_of(rows, ty):
+    lane = lax.broadcasted_iota(jnp.int32, (rows.shape[0], LANES), 1)
+    chunks = []
+    for t in (2 * ty, 2 * ty + 1):
+        tile, shift = divmod(t * CHUNK, LANES)
+        first = rows[:, tile * LANES : (tile + 1) * LANES]
+        if shift:
+            first = pltpu.roll(first, LANES - shift, 1)
+        if shift > LANES - CHUNK:
+            second = rows[:, (tile + 1) * LANES : (tile + 2) * LANES]
+            second = pltpu.roll(second, LANES - shift, 1)
+            first = jnp.where(lane < LANES - shift, first, second)
+        chunks.append(jnp.where(lane < CHUNK, first, 0.0))
+    return jnp.concatenate(chunks, axis=1)
+
+
+def spread_kernel(moved_ref, out_ref):
+    cells = moved_ref[:, 96:120, :].astype(F32)
+    cells = jnp.concatenate(
+        [cells[:, b * 4 : b * 4 + 4, :].reshape(64, LANES) for b in range(6)], axis=1
+    ).astype(BF16)
+    for ty in range(8):
+        out_ref[ty] = cells
+
+
+def bridge_kernel(cells_ref, moved_ref, out_ref):
+    weight = jnp.concatenate(
+        [moved_ref[:, c * 48 : c * 48 + 48, :].reshape(768, LANES) for c in range(2)], axis=1
+    )
+    sums = jnp.dot(cells_ref[...], weight, preferred_element_type=F32).astype(BF16)
     for y in range(8):
         for dy in range(3):
             source = min(max(y + dy - 1, 0), 7)
@@ -54,21 +116,33 @@
         gained_ref[:, lanes] = (total * gain_ref[:, lanes]).astype(BF16)
 
 
-def project_kernel(gained_ref, weights_ref, project_ref, out_weight_ref):
+def project_kernel(gained_ref, shards_hbm, project_ref, weights_ref, sems):
+    copies = []
+    for k in range(4):
+        part = pl.ds(4 * k, 4)
+        copies.append(
+            pltpu.make_async_copy(shards_hbm.at[part, pl.ds(0, LANES), :], weights_ref.at[part], sems.at[k])
+        )
+        copies[k].start()
     total = jnp.zeros(project_ref.shape, F32)
-    for t in range(CHUNKS):
+    for k in range(4):
+        copies[k].wait()
         total = total + jnp.dot(
-            gained_ref[:, t * LANES : (t + 1) * LANES],
-            weights_ref[t, 48:176, :],
+            gained_ref[:, k * 512 : (k + 1) * 512],
+            weights_ref[4 * k : 4 * k + 4].reshape(512, 768),
             preferred_element_type=F32,
         )
     project_ref[...] = total.astype(BF16)
+
+
+def rows_kernel(weights_hbm, after_ref, out_ref, weights_ref, sem):
+    copy = pltpu.make_async_copy(weights_hbm.at[:, pl.ds(LANES, 48), :], weights_ref, sem)
+    copy.start()
+    copy.wait()
     for t in range(CHUNKS):
         for b in range(6):
             rows = 48 if b < 5 else 16
-            out_weight_ref[t, b * 48 : b * 48 + rows, :] = weights_ref[
-                t, 0:rows, b * LANES : (b + 1) * LANES
-            ]
+            out_ref[t, b * 48 : b * 48 + rows, :] = weights_ref[t, 0:rows, b * LANES : (b + 1) * LANES]
 
 
 def axis_weight(fine, cell, low, high):
@@ -130,7 +204,8 @@
         & (col >= -place_ref[4])
         & (col < 8 + place_ref[5])
     )
-    bias_ref[...] = jnp.where(allowed, 0.0, NEG)
+    lane = lax.broadcasted_iota(jnp.int32, (1024, LANES), 1)
+    bias_ref[...] = jnp.where(((lane & (HD - 1)) == 0) & ~allowed, NEG, 0.0)
 
 
 def attend_kernel(
@@ -138,35 +213,42 @@
 ):
     patch = jnp.concatenate([left_ref[0], own_ref[0], right_ref[0]], axis=0)
     fine = jnp.dot(keys_ref[...], patch, preferred_element_type=F32)
+    query = jnp.dot(query_ref[...], patch, preferred_element_type=F32)
     scale = key_scale_ref[...]
+    query_scale = query_scale_ref[...] * (HD ** (-0.5) * 1.4426950408889634)
     bias = bias_ref[...]
-    first = fine[:, 0:128] * scale
-    second = fine[:, 128:256] * scale
-    third = fine[:, 256:384] * scale
-    lane = lax.broadcasted_iota(jnp.int32, (1024, LANES), 1)
-    low = lane < HD
-    key_0 = jnp.where(low, jnp.where(lane == 0, bias, 0.0), first).astype(BF16)
-    value_0 = jnp.where(low, second, 1.0).astype(BF16)
-    key_1 = jnp.where(low, third, jnp.where(lane == HD, bias, 0.0)).astype(BF16)
-    value_1 = jnp.where(low, 1.0, third).astype(BF16)
-    query = jnp.dot(query_ref[...], patch[:, 0:256], preferred_element_type=F32)
-    query_scale = query_scale_ref[...] * (HD ** (-0.5) * 1.4426950408889634)
-    query_lane = lax.broadcasted_iota(jnp.int32, (256, LANES), 1)
-    query_low = query_lane < HD
-    turned_0 = pltpu.roll(query[:, 0:128] * query_scale, HD, 1)
-    turned_1 = pltpu.roll(query[:, 128:256] * query_scale, HD, 1)
-    query_0 = jnp.where(query_low, jnp.where(query_lane == 0, 1.0, 0.0), turned_0).astype(BF16)
-    query_1 = jnp.where(query_low, turned_1, jnp.where(query_lane == HD, 1.0, 0.0)).astype(BF16)
-
-    def head(q, k, v):
-        scores = lax.dot_general(q, k, (((1,), (1,)), ((), ())), preferred_element_type=F32)
-        weights = jnp.exp2(scores - jnp.max(scores, axis=1, keepdims=True)).astype(BF16)
-        return jnp.dot(weights, v, preferred_element_type=F32)
-
-    mixed_0 = head(query_0, key_0, value_0)
-    mixed_1 = head(query_1, key_1, value_1)
-    mixed = jnp.where(query_low, mixed_0 / mixed_0[:, HD : HD + 1], mixed_1 / mixed_1[:, 0:1])
-    out_ref[0] = mixed.astype(BF16)
+    low = lax.broadcasted_iota(jnp.int32, (1024, LANES), 1) < HD
+    lane = lax.broadcasted_iota(jnp.int32, (256, LANES), 1)
+    query_low = lane < HD
+    scores = []
+    values = []
+    for pair in range(2):
+        start = pair * 384
+        first = fine[:, start : start + 128] * scale
+        second = fine[:, start + 128 : start + 256] * scale
+        third = fine[:, start + 256 : start + 384] * scale
+        turned_0 = pltpu.roll(query[:, start : start + 128] * query_scale, HD, 1)
+        turned_1 = pltpu.roll(query[:, start + 128 : start + 256] * query_scale, HD, 1)
+        query_0 = jnp.where(query_low, jnp.where(lane == 0, 1.0, 0.0), turned_0)
+        query_1 = jnp.where(query_low, turned_1, jnp.where(lane == HD, 1.0, 0.0))
+        key_0 = jnp.where(low, bias, first)
+        key_1 = jnp.where(low, third, bias)
+        for q, k in ((query_0, key_0), (query_1, key_1)):
+            scores.append(
+                lax.dot_general(
+                    q.astype(BF16), k.astype(BF16), (((1,), (1,)), ((), ())), preferred_element_type=F32
+                )
+            )
+        values.append(jnp.where(low, second, 1.0).astype(BF16))
+        values.append(jnp.where(low, 1.0, third).astype(BF16))
+    mixed = []
+    for score, value in zip(scores, values):
+        weights = jnp.exp2(score - jnp.max(score, axis=1, keepdims=True)).astype(BF16)
+        mixed.append(jnp.dot(weights, value, preferred_element_type=F32))
+    for pair in range(2):
+        head_0, head_1 = mixed[2 * pair], mixed[2 * pair + 1]
+        both = jnp.where(query_low, head_0 / head_0[:, HD : HD + 1], head_1 / head_1[:, 0:1])
+        out_ref[0, :, pair * LANES : (pair + 1) * LANES] = both.astype(BF16)
 
 
 def output_kernel(place_ref, attended_ref, hidden_ref, w0_ref, w1_ref, w2_ref, w3_ref, out_ref):
@@ -196,35 +278,37 @@
     rep = lax.axis_index("rep")
     smem = pl.BlockSpec(memory_space=pltpu.SMEM)
 
-    out_rows = jnp.pad(out_weight, ((0, 32), (0, LANES - CHUNK))).reshape(6, 48, LANES)
-    shard = jnp.concatenate(
-        [out_rows.transpose(1, 0, 2).reshape(48, 768), qkv_weight, jnp.zeros((8, 768), BF16)], axis=0
-    )
+    vmem = pl.BlockSpec(memory_space=pltpu.VMEM)
+    hbm = pl.BlockSpec(memory_space=pltpu.HBM)
+    message, shard = call(
+        start_kernel,
+        [jax.ShapeDtypeStruct((16, 120, LANES), BF16), jax.ShapeDtypeStruct((176, 768), BF16)],
+        58,
+        10,
+        500,
+        in_specs=[smem] + [hbm] * 4,
+        out_specs=[vmem, vmem],
+        scratch_shapes=[
+            pltpu.VMEM(latent.shape, BF16),
+            pltpu.VMEM(in_weight.shape, BF16),
+            pltpu.VMEM(qkv_weight.shape, BF16),
+            pltpu.VMEM((CHUNK, 256), BF16),
+            pltpu.SemaphoreType.DMA((4,)),
+        ],
+    )(ty.astype(jnp.int32).reshape(1), latent, in_weight, qkv_weight, out_weight.T)
     gathered = lax.all_gather(shard, "tx", axis=0)
-
-    source = lax.broadcasted_iota(jnp.int32, (WIDTH, 256), 0)
-    target = lax.broadcasted_iota(jnp.int32, (WIDTH, 256), 1)
-    inside = target & 127
-    pick = ((inside < CHUNK) & (source == ty * 240 + (target >> 7) * CHUNK + inside)).astype(BF16)
-    columns = jnp.dot(in_weight, pick, preferred_element_type=F32).astype(BF16)
-    columns = columns.reshape(3, 16, 256).transpose(1, 0, 2).reshape(1, 16, 768)
-    tiles = latent.reshape(2, 16, 2, 768).transpose(1, 0, 2, 3).reshape(16, 4, 768)
-    message = jnp.concatenate([jnp.broadcast_to(columns, (16, 16, 768)), tiles], axis=1)
     moved = lax.all_to_all(message, "tx", split_axis=0, concat_axis=0, tiled=True)
-    cells = moved[:, 16:20, :].reshape(1, 64, 768)
-    cells = lax.all_to_all(jnp.broadcast_to(cells, (8, 64, 768)), "ty", split_axis=0, concat_axis=0, tiled=True)
-    sums = call(
-        bridge_kernel,
-        jax.ShapeDtypeStruct((4, 8, 3, 16, 256), BF16),
-        16,
-        scratch_shapes=[pltpu.VMEM((768, 256), BF16)],
-    )(cells.reshape(512, 768), moved)
+    cells = call(spread_kernel, jax.ShapeDtypeStruct((8, 64, 768), BF16), 16, 10, 1500)(moved)
+    cells = lax.all_to_all(cells, "ty", split_axis=0, concat_axis=0, tiled=True)
+    sums = call(bridge_kernel, jax.ShapeDtypeStruct((4, 8, 3, 16, 256), BF16), 16, 800, 2000)(
+        cells.reshape(512, 768), moved
+    )
     parts = lax.all_to_all(
         sums.reshape(32, CELLS, 256), ("rep", "ty"), split_axis=0, concat_axis=0, tiled=True
     )
     gain = jnp.pad(norm_gain.astype(F32).reshape(CHUNKS, CHUNK), ((0, 0), (0, LANES - CHUNK))).reshape(1, WIDE)
     coarse, gained = call(
-        reduce_kernel, [jax.ShapeDtypeStruct((CELLS, WIDE), BF16)] * 2, 16
+        reduce_kernel, [jax.ShapeDtypeStruct((CELLS, WIDE), BF16)] * 2, 16, 100, 2000
     )(parts, gain)
 
     count = lax.axis_size("tx")
@@ -233,23 +317,7 @@
     coarse_left = lax.ppermute(coarse, "tx", to_right)
     coarse_right = lax.ppermute(coarse, "tx", to_left)
     gained = lax.all_gather(gained, "rep", axis=0, tiled=True)
-    project, own_rows = call(
-        project_kernel,
-        [jax.ShapeDtypeStruct((4 * CELLS, 768), BF16), jax.ShapeDtypeStruct((CHUNKS, 256, LANES), BF16)],
-        32,
-    )(gained, gathered)
-    project = lax.all_to_all(
-        project.reshape(4, CELLS, 768), "rep", split_axis=0, concat_axis=0, tiled=True
-    )
-    project_left = lax.ppermute(project, "tx", to_right)
-    project_right = lax.ppermute(project, "tx", to_left)
-
-    far_rows = lax.ppermute(own_rows, "rep", [(i, i ^ 2) for i in range(4)])
-    near_rows = lax.ppermute(own_rows, "rep", [(i, i ^ 1) for i in range(4)])
-    last_rows = lax.ppermute(far_rows, "rep", [(i, i ^ 1) for i in range(4)])
-
     place = jnp.concatenate([jnp.stack([ty, tx]).astype(jnp.int32), extents.reshape(4)])
-    vmem = pl.BlockSpec(memory_space=pltpu.VMEM)
     keys, query, key_scale, query_scale, bias, hidden = call(
         norm_kernel,
         [
@@ -261,20 +329,56 @@
             jax.ShapeDtypeStruct((256, WIDE), BF16),
         ],
         32,
+        2000,
+        8000,
         in_specs=[smem, vmem, vmem, vmem],
         out_specs=[vmem] * 6,
     )(place, coarse_left, coarse, coarse_right)
 
-    piece = pl.BlockSpec((1, CELLS, 384), lambda p: (p // 2, 0, p % 2))
+    anywhere = pl.BlockSpec(memory_space=pl.ANY)
+    project = call(
+        project_kernel,
+        jax.ShapeDtypeStruct((4 * CELLS, 768), BF16),
+        57,
+        1000,
+        6000,
+        in_specs=[vmem, hbm],
+        out_specs=vmem,
+        scratch_shapes=[pltpu.VMEM((CHUNKS, LANES, 768), BF16), pltpu.SemaphoreType.DMA((4,))],
+    )(gained, gathered)
+    own_rows = call(
+        rows_kernel,
+        jax.ShapeDtypeStruct((CHUNKS, 256, LANES), BF16),
+        57,
+        3000,
+        3000,
+        in_specs=[hbm, anywhere],
+        out_specs=vmem,
+        scratch_shapes=[pltpu.VMEM((CHUNKS, 48, 768), BF16), pltpu.SemaphoreType.DMA],
+    )(gathered, project)
+    project = lax.all_to_all(
+        project.reshape(4, CELLS, 768), "rep", split_axis=0, concat_axis=0, tiled=True
+    )
+    project_left = lax.ppermute(project, "tx", to_right)
+    project_right = lax.ppermute(project, "tx", to_left)
+
+    near_rows = lax.ppermute(own_rows, "rep", [(i, i ^ 1) for i in range(4)])
+    far_rows = lax.ppermute(own_rows, "rep", [(i, i ^ 2) for i in range(4)])
+    last_rows = lax.ppermute(
+        own_rows, ("rep", "ty"), [(r * 8 + y, (r ^ 3) * 8 + (y ^ 4)) for r in range(4) for y in range(8)]
+    )
 
     def whole(shape):
         return pl.BlockSpec(shape, lambda p: (0, 0))
 
+    piece = pl.BlockSpec((1, CELLS, 768), lambda p: (p, 0, 0))
     attended = call(
         attend_kernel,
         jax.ShapeDtypeStruct((4, 256, 256), BF16),
-        32,
-        grid=(8,),
+        48,
+        8000,
+        1000,
+        grid=(4,),
         in_specs=[
             piece,
             piece,
@@ -285,13 +389,15 @@
             whole((256, LANES)),
             whole((1024, LANES)),
         ],
-        out_specs=pl.BlockSpec((1, 256, LANES), lambda p: (p // 2, 0, p % 2)),
+        out_specs=pl.BlockSpec((1, 256, 256), lambda p: (p, 0, 0)),
     )(project_left, project, project_right, keys, query, key_scale, query_scale, bias)
 
     result = call(
         output_kernel,
         jax.ShapeDtypeStruct((256, WIDTH), BF16),
         32,
+        1000,
+        6000,
         in_specs=[smem] + [vmem] * 6,
         out_specs=vmem,
     )(rep.astype(jnp.int32).reshape(1), attended, hidden, own_rows, near_rows, far_rows, last_rows)

time: 204 us -> 162 us (0.79)
  waiting for transfers between devices: 51.6 us -> 18.5 us
  blocking collectives: 80.9 us -> 71.5 us
  starting transfers between devices: 23 us -> 31.8 us
  local copies, waits for them, and re-layouts: 4.63 us -> 0.11 us
    ppermute x1, waiting for transfers between devices: 22.5 us -> 3.11 us  [body(): far_rows = lax.ppermute(own_rows, 'rep', [(i, i ^ 2) for i in range(4)])]
    ppermute x1, waiting for transfers between devices: 12.6 us -> 0.01 us  [body(): coarse_right = lax.ppermute(coarse, 'tx', to_left)]
    all_to_all x1, blocking collectives: 56.4 us -> 47 us  [body(): lax.all_to_all(message, 'tx', split_axis=0, concat_axis=0, tiled=True)]
    all_to_all x1, waiting for transfers between devices: 4.21 us -> 0.01 us  [body(): lax.all_to_all(project.reshape(4, CELLS, 768), 'rep', split_axis=0, conca...]
    ppermute x1, starting transfers between devices: 1.91 us -> 5.76 us  [body(): lax.ppermute(own_rows, ('rep', 'ty'), [(r * 8 + y, (r ^ 3) * 8 + (y ^ 4))...]
    unnamed x10 -> x6, local copies, waits for them, and re-layouts: 3.22 us -> 0.02 us
    ppermute x1, starting transfers between devices: 2.13 us -> 5.24 us  [body(): coarse_left = lax.ppermute(coarse, 'tx', to_right)]
    ppermute x1, starting transfers between devices: 2.13 us -> 4.56 us  [body(): project_left = lax.ppermute(project, 'tx', to_right)]
  transfers between devices with their start and end apart: 10 -> 10, of which waited for: 4 -> 5; matrix products, arithmetic and copies ran while one was open for 1% -> 0% of each run, Pallas kernels for 10% -> 13%
where the time goes in v3:
time: 162 us; the launch traced here: 161 us
  blocking collectives  71.5 us (44%)
  starting transfers between devices  31.8 us (20%)
  Pallas kernels  25.5 us (16%)
  waiting for transfers between devices  18.5 us (11%)
  between operations  13.6 us (8%)
    all_to_all x1, blocking collectives, body(): lax.all_to_all(message, 'tx', split_axis=0, concat_axis=0, tiled=True)  47 us
    all_to_all x1, blocking collectives, body(): cells = lax.all_to_all(cells, 'ty', split_axis=0, concat_axis=0, tiled=True)  16 us
    all_to_all x1, waiting for transfers between devices, body(): lax.all_to_all(sums.reshape(32, CELLS, 256), ('rep', 'ty'), split_axis=0,...  12.2 us
    all_gather x1, blocking collectives, body(): gained = lax.all_gather(gained, 'rep', axis=0, tiled=True)  8.38 us
    pallas_call x1, Pallas kernels, body(): call(attend_kernel, jax.ShapeDtypeStruct((4, 256, 256), BF16), 48, 8000,...  8.02 us
    all_to_all x1, starting transfers between devices, body(): lax.all_to_all(sums.reshape(32, CELLS, 256), ('rep', 'ty'), split_axis=0,...  6 us
    ppermute x1, starting transfers between devices, body(): lax.ppermute(own_rows, ('rep', 'ty'), [(r * 8 + y, (r ^ 3) * 8 + (y ^ 4))...  5.76 us
    ppermute x1, starting transfers between devices, body(): coarse_left = lax.ppermute(coarse, 'tx', to_right)  5.24 us
  transfers between devices with their start and end apart: 10, of which 5 were waited for; matrix products, arithmetic and copies ran while one was open for 0% of the time, Pallas kernels for 13%

profile of v3, /device:TPU:24, one launch (start us, length us, event | category | flops | bytes accessed | tf_op | source)
XLA Modules:
  0.0 161.1 jit_solution(16106093463201767153)
XLA Ops:
  6.5 2.1 %shard_map.64 = (bf16[16,120,128]{2,1,0:T(8,128)(2,1)}, bf16[176,768]{1,0:T(8,128)(2,1)}) custom-call(s32[1]{0:T(128)} %bitcast.1.place_ref, bf16[1,2,32,768]{3,2,1,0:T(8,128)(2,1)} %latent_hbm.1, bf16[48,1920]{1,0:T(8,128)(2,1)} %weight_hbm.1, bf16[120,768]{1,0:T(8,128)(2,1)} %qkv_hbm.1, bf16[120,256]{1,0:T(8,128)(2,1)} %bitcast.16), custom_call_target="tpu_custom_call" | custom-call | flops 10000000 | bytes 500000 | tf_op jit(solution)/shard_map/pallas_call | solution.py:283
  8.7 47.0 %all_to_all.20.moved_ref = bf16[16,120,128]{2,1,0:T(8,128)(2,1)S(1)} all-to-all(bf16[16,120,128]{2,1,0:T(8,128)(2,1)} %get-tuple-element.15), channel_id=1, replica_groups=mesh['rep'=4,'ty'=8,'tx'=16] {'tx'}, dimensions={0} | all-to-all | bytes 983040 | tf_op jit(solution)/shard_map/all_to_all | solution.py:300
  55.8 16.0 %all_to_all.21 = bf16[8,64,768]{2,1,0:T(8,128)(2,1)S(1)} all-to-all(bf16[8,64,768]{2,1,0:T(8,128)(2,1)S(1)} %shard_map.65), channel_id=1, replica_groups=mesh['rep'=4,'ty'=8,'tx'=16] {'ty'}, dimensions={0} | all-to-all | bytes 1572864 | tf_op jit(solution)/shard_map/all_to_all | solution.py:302
  71.8 1.3 shard_map.66
  73.1 6.0 %all-to-all-start.2 = ((bf16[32,48,256]{2,1,0:T(8,128)(2,1)}), bf16[32,48,256]{2,1,0:T(8,128)(2,1)S(1)}, u32[]{:S(2)}, u32[]{:S(2)}) async-start(bf16[32,48,256]{2,1,0:T(8,128)(2,1)} %bitcast.4), calls=%async_computation.2 | async-start | bytes 1572864 | tf_op jit(solution)/shard_map/all_to_all | solution.py:306
  79.2 12.2 %all-to-all-done.2.parts_ref = bf16[32,48,256]{2,1,0:T(8,128)(2,1)S(1)} async-done(((bf16[32,48,256]{2,1,0:T(8,128)(2,1)}), bf16[32,48,256]{2,1,0:T(8,128)(2,1)S(1)}, u32[]{:S(2)}, u32[]{:S(2)}) %all-to-all-start.2) | async-done | bytes 786464 | tf_op jit(solution)/shard_map/all_to_all | solution.py:306
  91.4 0.8 shard_map.67
  92.2 1.3 collective-permute-start.3
  93.5 5.2 %collective-permute-start.2 = (bf16[48,2048]{1,0:T(8,128)(2,1)}, bf16[48,2048]{1,0:T(8,128)(2,1)}, u32[]{:S(2)}, u32[]{:S(2)}) collective-permute-start(bf16[48,2048]{1,0:T(8,128)(2,1)} %get-tuple-element.18.own_ref), channel_id=1, source_target_pairs={{0,1},{1,2},{2,3},{3,4},{4,5},{5,6},{6,7},{7,8},{8,9},{9,10},{10,1... | collective-permute-start | bytes 589832 | tf_op jit(solution)/shard_map/ppermute | solution.py:317
  98.8 8.4 %all_gather.9.gained_ref = bf16[192,2048]{1,0:T(8,128)(2,1)} all-gather(bf16[48,2048]{1,0:T(8,128)(2,1)S(1)} %get-tuple-element.16), channel_id=1, replica_groups=mesh['rep'=4,'ty'=8,'tx'=16] {'rep'}, dimensions={0}, use_global_device_ids=true | all-gather | bytes 983040 | tf_op jit(solution)/shard_map/all_gather | solution.py:319
  107.2 1.2 all-gather.3.cloned.1.call-done
  108.4 4.3 %shard_map.68.after_ref = bf16[192,768]{1,0:T(8,128)(2,1)} custom-call(bf16[192,2048]{1,0:T(8,128)(2,1)} %all_gather.9.gained_ref, bf16[16,176,768]{2,1,0:T(8,128)(2,1)} %bitcast.13), custom_call_target="tpu_custom_call" | custom-call | flops 1000000000 | bytes 6000000 | tf_op jit(solution)/shard_map/pallas_call | solution.py:339
  112.7 3.5 %all-to-all-start.3 = ((bf16[4,48,768]{2,1,0:T(8,128)(2,1)}), bf16[4,48,768]{2,1,0:T(8,128)(2,1)S(1)}, u32[]{:S(2)}, u32[]{:S(2)}) async-start(bf16[4,48,768]{2,1,0:T(8,128)(2,1)} %bitcast.15), calls=%async_computation.3 | async-start | bytes 589824 | tf_op jit(solution)/shard_map/all_to_all | solution.py:359
  116.2 2.5 %shard_map.71.w0_ref = bf16[16,256,128]{2,1,0:T(8,128)(2,1)} custom-call(bf16[16,176,768]{2,1,0:T(8,128)(2,1)} %bitcast.14, bf16[192,768]{1,0:T(8,128)(2,1)} %shard_map.68.after_ref), custom_call_target="tpu_custom_call" | custom-call | flops 3000000000 | bytes 3000000 | tf_op jit(solution)/shard_map/pallas_call | solution.py:349
  118.6 5.8 %collective-permute-start.6 = (bf16[16,256,128]{2,1,0:T(8,128)(2,1)}, bf16[16,256,128]{2,1,0:T(8,128)(2,1)S(1)}, u32[]{:S(2)}, u32[]{:S(2)}) collective-permute-start(bf16[16,256,128]{2,1,0:T(8,128)(2,1)} %shard_map.71.w0_ref), channel_id=1, source_target_pairs={{0,448},{16,464},{32,480},{48,496},{64,384},{80,400},{96,416},{112... | collective-permute-start | bytes 3145736 | tf_op jit(solution)/shard_map/ppermute | solution.py:367
  124.4 1.9 %collective-permute-start.5 = (bf16[16,256,128]{2,1,0:T(8,128)(2,1)}, bf16[16,256,128]{2,1,0:T(8,128)(2,1)S(1)}, u32[]{:S(2)}, u32[]{:S(2)}) collective-permute-start(bf16[16,256,128]{2,1,0:T(8,128)(2,1)} %shard_map.71.w0_ref), channel_id=1, source_target_pairs={{0,256},{128,384},{256,0},{384,128},{1,257},{129,385},{257,1},{385... | collective-permute-start | bytes 3145736 | tf_op jit(solution)/shard_map/ppermute | solution.py:366
  126.3 2.3 %collective-permute-start.4 = (bf16[16,256,128]{2,1,0:T(8,128)(2,1)}, bf16[16,256,128]{2,1,0:T(8,128)(2,1)S(1)}, u32[]{:S(2)}, u32[]{:S(2)}) collective-permute-start(bf16[16,256,128]{2,1,0:T(8,128)(2,1)} %shard_map.71.w0_ref), channel_id=1, source_target_pairs={{0,128},{128,0},{256,384},{384,256},{1,129},{129,1},{257,385},{385... | collective-permute-start | bytes 3145736 | tf_op jit(solution)/shard_map/ppermute | solution.py:365
  128.6 1.3 collective-permute-start.1
  129.9 4.6 %collective-permute-start = (bf16[4,48,768]{2,1,0:T(8,128)(2,1)S(1)}, bf16[4,48,768]{2,1,0:T(8,128)(2,1)S(1)}, u32[]{:S(2)}, u32[]{:S(2)}) collective-permute-start(bf16[4,48,768]{2,1,0:T(8,128)(2,1)S(1)} %all-to-all-done.3.own_ref), channel_id=1, source_target_pairs={{0,1},{1,2},{2,3},{3,4},{4,5},{5,6},{6,7},{7,8},{8,9},{9,10},{10,1... | collective-permute-start | bytes 884744 | tf_op jit(solution)/shard_map/ppermute | solution.py:362
  134.6 4.2 %shard_map.69 = (bf16[1024,144]{1,0:T(8,128)(2,1)S(1)}, bf16[256,144]{1,0:T(8,128)(2,1)S(1)}, f32[1024,128]{1,0:T(8,128)S(1)}, f32[256,128]{1,0:T(8,128)S(1)}, f...) custom-call(s32[6]{0:T(128)S(1)} %pad_add_fusion.place_ref, bf16[48,2048]{1,0:T(8,128)(2,1)} %collective-permute-done.2.left_ref, ...), custom_call_target="tpu_custom_call" | custom-call | flops 2000000000 | bytes 8000000 | tf_op jit(solution)/shard_map/pallas_call | solution.py:321
  139.6 1.2 collective-permute-done.left_ref
  140.8 8.0 %shard_map.70.attended_ref = bf16[4,256,256]{2,1,0:T(8,128)(2,1)S(1)} custom-call(bf16[4,48,768]{2,1,0:T(8,128)(2,1)S(1)} %collective-permute-done.left_ref, bf16[4,48,768]{2,1,0:T(8,128)(2,1)S(1)} %all-to-all-done.3.own_ref, bf16[4,48,768]{2,1,0:T(8,128)(2,1)S(1)} %collective-permute-done.1.right_ref, bf16[1024,144]{1,0:T(8,128)(2,1)S(1)} %get-tuple-element.19.keys_ref, ...), custom_call_target="tpu_custom_call" | custom-call | flops 8000000000 | bytes 1000000 | tf_op jit(solution)/shard_map/pallas_call | solution.py:375
  148.8 3.1 %collective-permute-done.5.w2_ref = bf16[16,256,128]{2,1,0:T(8,128)(2,1)S(1)} collective-permute-done((bf16[16,256,128]{2,1,0:T(8,128)(2,1)}, bf16[16,256,128]{2,1,0:T(8,128)(2,1)S(1)}, u32[]{:S(2)}, u32[]{:S(2)}) %collective-permute-start.5) | collective-permute-done | bytes 1048608 | tf_op jit(solution)/shard_map/ppermute | solution.py:366
  151.9 2.3 %shard_map.72 = bf16[256,1920]{1,0:T(8,128)(2,1)} custom-call(s32[1]{0:T(128)} %bitcast.place_ref, bf16[4,256,256]{2,1,0:T(8,128)(2,1)S(1)} %shard_map.70.attended_ref, bf16[256,2048]{1,0:T(8,128)(2,1)S(1)} %get-tuple-element.24.hidden_ref, bf16[16,256,128]{2,1,0:T(8,128)(2,1)S(1)} %copy-done, bf16[16,256,128]{2,1,0:T(8,128)(2,1)S(1)} %collective-permute-done.4.w1_ref, ...), custom_call_target="tpu_custom_call" | custom-call | flops 1000000000 | bytes 6000000 | tf_op jit(solution)/shard_map/pallas_call | solution.py:395
  (18 shorter events, 1.0 us)
Async XLA Ops:
  6.5 101.8 %all-gather.3.cloned.1.call-start = ((), (), s32[]{:S(2)}) async-start(), calls=%async_computation.4 | async-start | bytes 4595712 | tf_op jit(solution)/shard_map/all_gather | solution.py:299
  8.7 70.4 %copy-start.1 = (bf16[1920]{0:T(1024)(128)(2,1)S(1)}, bf16[1920]{0:T(1024)(128)(2,1)}, u32[]{:S(2)}) copy-start(bf16[1920]{0:T(1024)(128)(2,1)} %param.10) | copy-start | bytes 11524
  73.1 18.4 %all-to-all-start.2 = ((bf16[32,48,256]{2,1,0:T(8,128)(2,1)}), bf16[32,48,256]{2,1,0:T(8,128)(2,1)S(1)}, u32[]{:S(2)}, u32[]{:S(2)}) async-start(bf16[32,48,256]{2,1,0:T(8,128)(2,1)} %bitcast.4), calls=%async_computation.2 | async-start | bytes 1572864 | tf_op jit(solution)/shard_map/all_to_all | solution.py:306
  92.2 36.4 %collective-permute-start.3 = (bf16[48,2048]{1,0:T(8,128)(2,1)}, bf16[48,2048]{1,0:T(8,128)(2,1)}, u32[]{:S(2)}, u32[]{:S(2)}) collective-permute-start(bf16[48,2048]{1,0:T(8,128)(2,1)} %get-tuple-element.18.own_ref), channel_id=1, source_target_pairs={{1,0},{2,1},{3,2},{4,3},{5,4},{6,5},{7,6},{8,7},{9,8},{10,9},{11,1... | collective-permute-start | bytes 589832 | tf_op jit(solution)/shard_map/ppermute | solution.py:318
  93.5 36.4 %collective-permute-start.2 = (bf16[48,2048]{1,0:T(8,128)(2,1)}, bf16[48,2048]{1,0:T(8,128)(2,1)}, u32[]{:S(2)}, u32[]{:S(2)}) collective-permute-start(bf16[48,2048]{1,0:T(8,128)(2,1)} %get-tuple-element.18.own_ref), channel_id=1, source_target_pairs={{0,1},{1,2},{2,3},{3,4},{4,5},{5,6},{6,7},{7,8},{8,9},{9,10},{10,1... | collective-permute-start | bytes 589832 | tf_op jit(solution)/shard_map/ppermute | solution.py:317
  112.7 15.9 %all-to-all-start.3 = ((bf16[4,48,768]{2,1,0:T(8,128)(2,1)}), bf16[4,48,768]{2,1,0:T(8,128)(2,1)S(1)}, u32[]{:S(2)}, u32[]{:S(2)}) async-start(bf16[4,48,768]{2,1,0:T(8,128)(2,1)} %bitcast.15), calls=%async_computation.3 | async-start | bytes 589824 | tf_op jit(solution)/shard_map/all_to_all | solution.py:359
  116.2 18.4 %copy-start.2 = (s32[1,1,4]{2,1,0:T(1,128)S(1)}, s32[1,1,4]{2,1,0:T(1,128)}, u32[]{:S(2)}) copy-start(s32[1,1,4]{2,1,0:T(1,128)} %param.11) | copy-start | bytes 52
  118.6 30.2 %collective-permute-start.6 = (bf16[16,256,128]{2,1,0:T(8,128)(2,1)}, bf16[16,256,128]{2,1,0:T(8,128)(2,1)S(1)}, u32[]{:S(2)}, u32[]{:S(2)}) collective-permute-start(bf16[16,256,128]{2,1,0:T(8,128)(2,1)} %shard_map.71.w0_ref), channel_id=1, source_target_pairs={{0,448},{16,464},{32,480},{48,496},{64,384},{80,400},{96,416},{112... | collective-permute-start | bytes 3145736 | tf_op jit(solution)/shard_map/ppermute | solution.py:367
  124.4 27.5 %collective-permute-start.5 = (bf16[16,256,128]{2,1,0:T(8,128)(2,1)}, bf16[16,256,128]{2,1,0:T(8,128)(2,1)S(1)}, u32[]{:S(2)}, u32[]{:S(2)}) collective-permute-start(bf16[16,256,128]{2,1,0:T(8,128)(2,1)} %shard_map.71.w0_ref), channel_id=1, source_target_pairs={{0,256},{128,384},{256,0},{384,128},{1,257},{129,385},{257,1},{385... | collective-permute-start | bytes 3145736 | tf_op jit(solution)/shard_map/ppermute | solution.py:366
  126.3 25.6 %collective-permute-start.4 = (bf16[16,256,128]{2,1,0:T(8,128)(2,1)}, bf16[16,256,128]{2,1,0:T(8,128)(2,1)S(1)}, u32[]{:S(2)}, u32[]{:S(2)}) collective-permute-start(bf16[16,256,128]{2,1,0:T(8,128)(2,1)} %shard_map.71.w0_ref), channel_id=1, source_target_pairs={{0,128},{128,0},{256,384},{384,256},{1,129},{129,1},{257,385},{385... | collective-permute-start | bytes 3145736 | tf_op jit(solution)/shard_map/ppermute | solution.py:365
  128.6 11.0 %collective-permute-start.1 = (bf16[4,48,768]{2,1,0:T(8,128)(2,1)S(1)}, bf16[4,48,768]{2,1,0:T(8,128)(2,1)S(1)}, u32[]{:S(2)}, u32[]{:S(2)}) collective-permute-start(bf16[4,48,768]{2,1,0:T(8,128)(2,1)S(1)} %all-to-all-done.3.own_ref), channel_id=1, source_target_pairs={{1,0},{2,1},{3,2},{4,3},{5,4},{6,5},{7,6},{8,7},{9,8},{10,9},{11,1... | collective-permute-start | bytes 884744 | tf_op jit(solution)/shard_map/ppermute | solution.py:363
  129.9 10.8 %collective-permute-start = (bf16[4,48,768]{2,1,0:T(8,128)(2,1)S(1)}, bf16[4,48,768]{2,1,0:T(8,128)(2,1)S(1)}, u32[]{:S(2)}, u32[]{:S(2)}) collective-permute-start(bf16[4,48,768]{2,1,0:T(8,128)(2,1)S(1)} %all-to-all-done.3.own_ref), channel_id=1, source_target_pairs={{0,1},{1,2},{2,3},{3,4},{4,5},{5,6},{6,7},{7,8},{8,9},{9,10},{10,1... | collective-permute-start | bytes 884744 | tf_op jit(solution)/shard_map/ppermute | solution.py:362
  140.8 11.2 %copy-start = (bf16[16,256,128]{2,1,0:T(8,128)(2,1)S(1)}, bf16[16,256,128]{2,1,0:T(8,128)(2,1)}, u32[]{:S(2)}) copy-start(bf16[16,256,128]{2,1,0:T(8,128)(2,1)} %shard_map.71.w0_ref) | copy-start | bytes 3145732
Sparse Core Ops, SparseCore 0:
  9.4 98.8 all-gather.2

commit v4 on v3

--- a/solution.py
+++ b/solution.py
@@ -135,11 +135,17 @@
     project_ref[...] = total.astype(BF16)
 
 
-def rows_kernel(weights_hbm, after_ref, out_ref, weights_ref, sem):
-    copy = pltpu.make_async_copy(weights_hbm.at[:, pl.ds(LANES, 48), :], weights_ref, sem)
-    copy.start()
-    copy.wait()
+def rows_kernel(weights_hbm, after_ref, out_ref, weights_ref, sems):
+    copies = []
+    for k in range(4):
+        part = pl.ds(4 * k, 4)
+        copies.append(
+            pltpu.make_async_copy(weights_hbm.at[part, pl.ds(LANES, 48), :], weights_ref.at[part], sems.at[k])
+        )
+        copies[k].start()
     for t in range(CHUNKS):
+        if t % 4 == 0:
+            copies[t // 4].wait()
         for b in range(6):
             rows = 48 if b < 5 else 16
             out_ref[t, b * 48 : b * 48 + rows, :] = weights_ref[t, 0:rows, b * LANES : (b + 1) * LANES]
@@ -220,8 +226,7 @@
     low = lax.broadcasted_iota(jnp.int32, (1024, LANES), 1) < HD
     lane = lax.broadcasted_iota(jnp.int32, (256, LANES), 1)
     query_low = lane < HD
-    scores = []
-    values = []
+    heads = []
     for pair in range(2):
         start = pair * 384
         first = fine[:, start : start + 128] * scale
@@ -229,26 +234,27 @@
         third = fine[:, start + 256 : start + 384] * scale
         turned_0 = pltpu.roll(query[:, start : start + 128] * query_scale, HD, 1)
         turned_1 = pltpu.roll(query[:, start + 128 : start + 256] * query_scale, HD, 1)
-        query_0 = jnp.where(query_low, jnp.where(lane == 0, 1.0, 0.0), turned_0)
-        query_1 = jnp.where(query_low, turned_1, jnp.where(lane == HD, 1.0, 0.0))
-        key_0 = jnp.where(low, bias, first)
-        key_1 = jnp.where(low, third, bias)
-        for q, k in ((query_0, key_0), (query_1, key_1)):
-            scores.append(
-                lax.dot_general(
-                    q.astype(BF16), k.astype(BF16), (((1,), (1,)), ((), ())), preferred_element_type=F32
-                )
-            )
-        values.append(jnp.where(low, second, 1.0).astype(BF16))
-        values.append(jnp.where(low, 1.0, third).astype(BF16))
-    mixed = []
-    for score, value in zip(scores, values):
-        weights = jnp.exp2(score - jnp.max(score, axis=1, keepdims=True)).astype(BF16)
-        mixed.append(jnp.dot(weights, value, preferred_element_type=F32))
-    for pair in range(2):
-        head_0, head_1 = mixed[2 * pair], mixed[2 * pair + 1]
-        both = jnp.where(query_low, head_0 / head_0[:, HD : HD + 1], head_1 / head_1[:, 0:1])
-        out_ref[0, :, pair * LANES : (pair + 1) * LANES] = both.astype(BF16)
+        query_0 = jnp.where(query_low, jnp.where(lane == 0, 1.0, 0.0), turned_0).astype(BF16)
+        query_1 = jnp.where(query_low, turned_1, jnp.where(lane == HD, 1.0, 0.0)).astype(BF16)
+        key_0 = jnp.where(low, bias, first).astype(BF16)
+        key_1 = jnp.where(low, third, bias).astype(BF16)
+        value_0 = jnp.where(low, second, 1.0).astype(BF16)
+        value_1 = jnp.where(low, 1.0, third).astype(BF16)
+        heads += [(query_0, key_0, value_0), (query_1, key_1, value_1)]
+    block_low = query_low[0:128]
+    for start in (0, 128):
+        rows = slice(start, start + 128)
+        scores = [
+            lax.dot_general(q[rows], k, (((1,), (1,)), ((), ())), preferred_element_type=F32) for q, k, _ in heads
+        ]
+        mixed = []
+        for score, (_, _, value) in zip(scores, heads):
+            weights = jnp.exp2(score - jnp.max(score, axis=1, keepdims=True)).astype(BF16)
+            mixed.append(jnp.dot(weights, value, preferred_element_type=F32))
+        for pair in range(2):
+            head_0, head_1 = mixed[2 * pair], mixed[2 * pair + 1]
+            both = jnp.where(block_low, head_0 / head_0[:, HD : HD + 1], head_1 / head_1[:, 0:1])
+            out_ref[0, rows, pair * LANES : (pair + 1) * LANES] = both.astype(BF16)
 
 
 def output_kernel(place_ref, attended_ref, hidden_ref, w0_ref, w1_ref, w2_ref, w3_ref, out_ref):
@@ -354,7 +360,7 @@
         3000,
         in_specs=[hbm, anywhere],
         out_specs=vmem,
-        scratch_shapes=[pltpu.VMEM((CHUNKS, 48, 768), BF16), pltpu.SemaphoreType.DMA],
+        scratch_shapes=[pltpu.VMEM((CHUNKS, 48, 768), BF16), pltpu.SemaphoreType.DMA((4,))],
     )(gathered, project)
     project = lax.all_to_all(
         project.reshape(4, CELLS, 768), "rep", split_axis=0, concat_axis=0, tiled=True

time: 162 us -> 162 us (level)
  no operation moved by 1% of the time
where the time goes in v4:
time: 162 us; the launch traced here: 161 us
  blocking collectives  71.5 us (44%)
  starting transfers between devices  31.8 us (20%)
  Pallas kernels  25.2 us (16%)
  waiting for transfers between devices  18.7 us (12%)
  between operations  13.6 us (8%)
    all_to_all x1, blocking collectives, body(): lax.all_to_all(message, 'tx', split_axis=0, concat_axis=0, tiled=True)  47 us
    all_to_all x1, blocking collectives, body(): cells = lax.all_to_all(cells, 'ty', split_axis=0, concat_axis=0, tiled=True)  16 us
    all_to_all x1, waiting for transfers between devices, body(): lax.all_to_all(sums.reshape(32, CELLS, 256), ('rep', 'ty'), split_axis=0,...  12.2 us
    all_gather x1, blocking collectives, body(): gained = lax.all_gather(gained, 'rep', axis=0, tiled=True)  8.38 us
    pallas_call x1, Pallas kernels, body(): call(attend_kernel, jax.ShapeDtypeStruct((4, 256, 256), BF16), 48, 8000,...  7.78 us
    all_to_all x1, starting transfers between devices, body(): lax.all_to_all(sums.reshape(32, CELLS, 256), ('rep', 'ty'), split_axis=0,...  6 us
    ppermute x1, starting transfers between devices, body(): lax.ppermute(own_rows, ('rep', 'ty'), [(r * 8 + y, (r ^ 3) * 8 + (y ^ 4))...  5.76 us
    ppermute x1, starting transfers between devices, body(): coarse_left = lax.ppermute(coarse, 'tx', to_right)  5.24 us
  transfers between devices with their start and end apart: 10, of which 5 were waited for; matrix products, arithmetic and copies ran while one was open for 0% of the time, Pallas kernels for 13%

profile of v4, /device:TPU:24, one launch (start us, length us, event | category | flops | bytes accessed | tf_op | source)
XLA Modules:
  0.0 160.9 jit_solution(13212223606945936400)
XLA Ops:
  6.5 2.1 %shard_map.64 = (bf16[16,120,128]{2,1,0:T(8,128)(2,1)}, bf16[176,768]{1,0:T(8,128)(2,1)}) custom-call(s32[1]{0:T(128)} %bitcast.1.place_ref, bf16[1,2,32,768]{3,2,1,0:T(8,128)(2,1)} %latent_hbm.1, bf16[48,1920]{1,0:T(8,128)(2,1)} %weight_hbm.1, bf16[120,768]{1,0:T(8,128)(2,1)} %qkv_hbm.1, bf16[120,256]{1,0:T(8,128)(2,1)} %bitcast.16), custom_call_target="tpu_custom_call" | custom-call | flops 10000000 | bytes 500000 | tf_op jit(solution)/shard_map/pallas_call | solution.py:289
  8.7 47.0 %all_to_all.20.moved_ref = bf16[16,120,128]{2,1,0:T(8,128)(2,1)S(1)} all-to-all(bf16[16,120,128]{2,1,0:T(8,128)(2,1)} %get-tuple-element.15), channel_id=1, replica_groups=mesh['rep'=4,'ty'=8,'tx'=16] {'tx'}, dimensions={0} | all-to-all | bytes 983040 | tf_op jit(solution)/shard_map/all_to_all | solution.py:306
  55.8 16.0 %all_to_all.21 = bf16[8,64,768]{2,1,0:T(8,128)(2,1)S(1)} all-to-all(bf16[8,64,768]{2,1,0:T(8,128)(2,1)S(1)} %shard_map.65), channel_id=1, replica_groups=mesh['rep'=4,'ty'=8,'tx'=16] {'ty'}, dimensions={0} | all-to-all | bytes 1572864 | tf_op jit(solution)/shard_map/all_to_all | solution.py:308
  71.8 1.3 shard_map.66
  73.1 6.0 %all-to-all-start.2 = ((bf16[32,48,256]{2,1,0:T(8,128)(2,1)}), bf16[32,48,256]{2,1,0:T(8,128)(2,1)S(1)}, u32[]{:S(2)}, u32[]{:S(2)}) async-start(bf16[32,48,256]{2,1,0:T(8,128)(2,1)} %bitcast.4), calls=%async_computation.2 | async-start | bytes 1572864 | tf_op jit(solution)/shard_map/all_to_all | solution.py:312
  79.2 12.2 %all-to-all-done.2.parts_ref = bf16[32,48,256]{2,1,0:T(8,128)(2,1)S(1)} async-done(((bf16[32,48,256]{2,1,0:T(8,128)(2,1)}), bf16[32,48,256]{2,1,0:T(8,128)(2,1)S(1)}, u32[]{:S(2)}, u32[]{:S(2)}) %all-to-all-start.2) | async-done | bytes 786464 | tf_op jit(solution)/shard_map/all_to_all | solution.py:312
  91.4 0.8 shard_map.67
  92.2 1.3 collective-permute-start.3
  93.5 5.2 %collective-permute-start.2 = (bf16[48,2048]{1,0:T(8,128)(2,1)}, bf16[48,2048]{1,0:T(8,128)(2,1)}, u32[]{:S(2)}, u32[]{:S(2)}) collective-permute-start(bf16[48,2048]{1,0:T(8,128)(2,1)} %get-tuple-element.18.own_ref), channel_id=1, source_target_pairs={{0,1},{1,2},{2,3},{3,4},{4,5},{5,6},{6,7},{7,8},{8,9},{9,10},{10,1... | collective-permute-start | bytes 589832 | tf_op jit(solution)/shard_map/ppermute | solution.py:323
  98.8 8.4 %all_gather.9.gained_ref = bf16[192,2048]{1,0:T(8,128)(2,1)} all-gather(bf16[48,2048]{1,0:T(8,128)(2,1)S(1)} %get-tuple-element.16), channel_id=1, replica_groups=mesh['rep'=4,'ty'=8,'tx'=16] {'rep'}, dimensions={0}, use_global_device_ids=true | all-gather | bytes 983040 | tf_op jit(solution)/shard_map/all_gather | solution.py:325
  107.2 1.2 all-gather.3.cloned.1.call-done
  108.4 4.3 %shard_map.68.after_ref = bf16[192,768]{1,0:T(8,128)(2,1)} custom-call(bf16[192,2048]{1,0:T(8,128)(2,1)} %all_gather.9.gained_ref, bf16[16,176,768]{2,1,0:T(8,128)(2,1)} %bitcast.13), custom_call_target="tpu_custom_call" | custom-call | flops 1000000000 | bytes 6000000 | tf_op jit(solution)/shard_map/pallas_call | solution.py:345
  112.7 3.5 %all-to-all-start.3 = ((bf16[4,48,768]{2,1,0:T(8,128)(2,1)}), bf16[4,48,768]{2,1,0:T(8,128)(2,1)S(1)}, u32[]{:S(2)}, u32[]{:S(2)}) async-start(bf16[4,48,768]{2,1,0:T(8,128)(2,1)} %bitcast.15), calls=%async_computation.3 | async-start | bytes 589824 | tf_op jit(solution)/shard_map/all_to_all | solution.py:365
  116.2 2.3 %shard_map.71.w0_ref = bf16[16,256,128]{2,1,0:T(8,128)(2,1)} custom-call(bf16[16,176,768]{2,1,0:T(8,128)(2,1)} %bitcast.14, bf16[192,768]{1,0:T(8,128)(2,1)} %shard_map.68.after_ref), custom_call_target="tpu_custom_call" | custom-call | flops 3000000000 | bytes 3000000 | tf_op jit(solution)/shard_map/pallas_call | solution.py:355
  118.5 5.8 %collective-permute-start.6 = (bf16[16,256,128]{2,1,0:T(8,128)(2,1)}, bf16[16,256,128]{2,1,0:T(8,128)(2,1)S(1)}, u32[]{:S(2)}, u32[]{:S(2)}) collective-permute-start(bf16[16,256,128]{2,1,0:T(8,128)(2,1)} %shard_map.71.w0_ref), channel_id=1, source_target_pairs={{0,448},{16,464},{32,480},{48,496},{64,384},{80,400},{96,416},{112... | collective-permute-start | bytes 3145736 | tf_op jit(solution)/shard_map/ppermute | solution.py:373
  124.3 1.9 %collective-permute-start.5 = (bf16[16,256,128]{2,1,0:T(8,128)(2,1)}, bf16[16,256,128]{2,1,0:T(8,128)(2,1)S(1)}, u32[]{:S(2)}, u32[]{:S(2)}) collective-permute-start(bf16[16,256,128]{2,1,0:T(8,128)(2,1)} %shard_map.71.w0_ref), channel_id=1, source_target_pairs={{0,256},{128,384},{256,0},{384,128},{1,257},{129,385},{257,1},{385... | collective-permute-start | bytes 3145736 | tf_op jit(solution)/shard_map/ppermute | solution.py:372
  126.2 2.3 %collective-permute-start.4 = (bf16[16,256,128]{2,1,0:T(8,128)(2,1)}, bf16[16,256,128]{2,1,0:T(8,128)(2,1)S(1)}, u32[]{:S(2)}, u32[]{:S(2)}) collective-permute-start(bf16[16,256,128]{2,1,0:T(8,128)(2,1)} %shard_map.71.w0_ref), channel_id=1, source_target_pairs={{0,128},{128,0},{256,384},{384,256},{1,129},{129,1},{257,385},{385... | collective-permute-start | bytes 3145736 | tf_op jit(solution)/shard_map/ppermute | solution.py:371
  128.5 1.3 collective-permute-start.1
  129.8 4.6 %collective-permute-start = (bf16[4,48,768]{2,1,0:T(8,128)(2,1)S(1)}, bf16[4,48,768]{2,1,0:T(8,128)(2,1)S(1)}, u32[]{:S(2)}, u32[]{:S(2)}) collective-permute-start(bf16[4,48,768]{2,1,0:T(8,128)(2,1)S(1)} %all-to-all-done.3.own_ref), channel_id=1, source_target_pairs={{0,1},{1,2},{2,3},{3,4},{4,5},{5,6},{6,7},{7,8},{8,9},{9,10},{10,1... | collective-permute-start | bytes 884744 | tf_op jit(solution)/shard_map/ppermute | solution.py:368
  134.5 4.3 %shard_map.69 = (bf16[1024,144]{1,0:T(8,128)(2,1)S(1)}, bf16[256,144]{1,0:T(8,128)(2,1)S(1)}, f32[1024,128]{1,0:T(8,128)S(1)}, f32[256,128]{1,0:T(8,128)S(1)}, f...) custom-call(s32[6]{0:T(128)S(1)} %pad_add_fusion.place_ref, bf16[48,2048]{1,0:T(8,128)(2,1)} %collective-permute-done.2.left_ref, ...), custom_call_target="tpu_custom_call" | custom-call | flops 2000000000 | bytes 8000000 | tf_op jit(solution)/shard_map/pallas_call | solution.py:327
  139.4 1.2 collective-permute-done.left_ref
  140.6 7.8 %shard_map.70.attended_ref = bf16[4,256,256]{2,1,0:T(8,128)(2,1)S(1)} custom-call(bf16[4,48,768]{2,1,0:T(8,128)(2,1)S(1)} %collective-permute-done.left_ref, bf16[4,48,768]{2,1,0:T(8,128)(2,1)S(1)} %all-to-all-done.3.own_ref, bf16[4,48,768]{2,1,0:T(8,128)(2,1)S(1)} %collective-permute-done.1.right_ref, bf16[1024,144]{1,0:T(8,128)(2,1)S(1)} %get-tuple-element.19.keys_ref, ...), custom_call_target="tpu_custom_call" | custom-call | flops 8000000000 | bytes 1000000 | tf_op jit(solution)/shard_map/pallas_call | solution.py:381
  148.4 3.4 %collective-permute-done.5.w2_ref = bf16[16,256,128]{2,1,0:T(8,128)(2,1)S(1)} collective-permute-done((bf16[16,256,128]{2,1,0:T(8,128)(2,1)}, bf16[16,256,128]{2,1,0:T(8,128)(2,1)S(1)}, u32[]{:S(2)}, u32[]{:S(2)}) %collective-permute-start.5) | collective-permute-done | bytes 1048608 | tf_op jit(solution)/shard_map/ppermute | solution.py:372
  151.8 2.3 %shard_map.72 = bf16[256,1920]{1,0:T(8,128)(2,1)} custom-call(s32[1]{0:T(128)} %bitcast.place_ref, bf16[4,256,256]{2,1,0:T(8,128)(2,1)S(1)} %shard_map.70.attended_ref, bf16[256,2048]{1,0:T(8,128)(2,1)S(1)} %get-tuple-element.24.hidden_ref, bf16[16,256,128]{2,1,0:T(8,128)(2,1)S(1)} %copy-done, bf16[16,256,128]{2,1,0:T(8,128)(2,1)S(1)} %collective-permute-done.4.w1_ref, ...), custom_call_target="tpu_custom_call" | custom-call | flops 1000000000 | bytes 6000000 | tf_op jit(solution)/shard_map/pallas_call | solution.py:401
  (18 shorter events, 1.0 us)
Async XLA Ops:
  6.5 101.8 %all-gather.3.cloned.1.call-start = ((), (), s32[]{:S(2)}) async-start(), calls=%async_computation.4 | async-start | bytes 4595712 | tf_op jit(solution)/shard_map/all_gather | solution.py:305
  8.7 70.4 %copy-start.1 = (bf16[1920]{0:T(1024)(128)(2,1)S(1)}, bf16[1920]{0:T(1024)(128)(2,1)}, u32[]{:S(2)}) copy-start(bf16[1920]{0:T(1024)(128)(2,1)} %param.10) | copy-start | bytes 11524
  73.1 18.4 %all-to-all-start.2 = ((bf16[32,48,256]{2,1,0:T(8,128)(2,1)}), bf16[32,48,256]{2,1,0:T(8,128)(2,1)S(1)}, u32[]{:S(2)}, u32[]{:S(2)}) async-start(bf16[32,48,256]{2,1,0:T(8,128)(2,1)} %bitcast.4), calls=%async_computation.2 | async-start | bytes 1572864 | tf_op jit(solution)/shard_map/all_to_all | solution.py:312
  92.2 36.2 %collective-permute-start.3 = (bf16[48,2048]{1,0:T(8,128)(2,1)}, bf16[48,2048]{1,0:T(8,128)(2,1)}, u32[]{:S(2)}, u32[]{:S(2)}) collective-permute-start(bf16[48,2048]{1,0:T(8,128)(2,1)} %get-tuple-element.18.own_ref), channel_id=1, source_target_pairs={{1,0},{2,1},{3,2},{4,3},{5,4},{6,5},{7,6},{8,7},{9,8},{10,9},{11,1... | collective-permute-start | bytes 589832 | tf_op jit(solution)/shard_map/ppermute | solution.py:324
  93.5 36.3 %collective-permute-start.2 = (bf16[48,2048]{1,0:T(8,128)(2,1)}, bf16[48,2048]{1,0:T(8,128)(2,1)}, u32[]{:S(2)}, u32[]{:S(2)}) collective-permute-start(bf16[48,2048]{1,0:T(8,128)(2,1)} %get-tuple-element.18.own_ref), channel_id=1, source_target_pairs={{0,1},{1,2},{2,3},{3,4},{4,5},{5,6},{6,7},{7,8},{8,9},{9,10},{10,1... | collective-permute-start | bytes 589832 | tf_op jit(solution)/shard_map/ppermute | solution.py:323
  112.7 15.8 %all-to-all-start.3 = ((bf16[4,48,768]{2,1,0:T(8,128)(2,1)}), bf16[4,48,768]{2,1,0:T(8,128)(2,1)S(1)}, u32[]{:S(2)}, u32[]{:S(2)}) async-start(bf16[4,48,768]{2,1,0:T(8,128)(2,1)} %bitcast.15), calls=%async_computation.3 | async-start | bytes 589824 | tf_op jit(solution)/shard_map/all_to_all | solution.py:365
  116.2 18.2 %copy-start.2 = (s32[1,1,4]{2,1,0:T(1,128)S(1)}, s32[1,1,4]{2,1,0:T(1,128)}, u32[]{:S(2)}) copy-start(s32[1,1,4]{2,1,0:T(1,128)} %param.11) | copy-start | bytes 52
  118.5 29.9 %collective-permute-start.6 = (bf16[16,256,128]{2,1,0:T(8,128)(2,1)}, bf16[16,256,128]{2,1,0:T(8,128)(2,1)S(1)}, u32[]{:S(2)}, u32[]{:S(2)}) collective-permute-start(bf16[16,256,128]{2,1,0:T(8,128)(2,1)} %shard_map.71.w0_ref), channel_id=1, source_target_pairs={{0,448},{16,464},{32,480},{48,496},{64,384},{80,400},{96,416},{112... | collective-permute-start | bytes 3145736 | tf_op jit(solution)/shard_map/ppermute | solution.py:373
  124.3 27.5 %collective-permute-start.5 = (bf16[16,256,128]{2,1,0:T(8,128)(2,1)}, bf16[16,256,128]{2,1,0:T(8,128)(2,1)S(1)}, u32[]{:S(2)}, u32[]{:S(2)}) collective-permute-start(bf16[16,256,128]{2,1,0:T(8,128)(2,1)} %shard_map.71.w0_ref), channel_id=1, source_target_pairs={{0,256},{128,384},{256,0},{384,128},{1,257},{129,385},{257,1},{385... | collective-permute-start | bytes 3145736 | tf_op jit(solution)/shard_map/ppermute | solution.py:372
  126.2 25.6 %collective-permute-start.4 = (bf16[16,256,128]{2,1,0:T(8,128)(2,1)}, bf16[16,256,128]{2,1,0:T(8,128)(2,1)S(1)}, u32[]{:S(2)}, u32[]{:S(2)}) collective-permute-start(bf16[16,256,128]{2,1,0:T(8,128)(2,1)} %shard_map.71.w0_ref), channel_id=1, source_target_pairs={{0,128},{128,0},{256,384},{384,256},{1,129},{129,1},{257,385},{385... | collective-permute-start | bytes 3145736 | tf_op jit(solution)/shard_map/ppermute | solution.py:371
  128.5 11.0 %collective-permute-start.1 = (bf16[4,48,768]{2,1,0:T(8,128)(2,1)S(1)}, bf16[4,48,768]{2,1,0:T(8,128)(2,1)S(1)}, u32[]{:S(2)}, u32[]{:S(2)}) collective-permute-start(bf16[4,48,768]{2,1,0:T(8,128)(2,1)S(1)} %all-to-all-done.3.own_ref), channel_id=1, source_target_pairs={{1,0},{2,1},{3,2},{4,3},{5,4},{6,5},{7,6},{8,7},{9,8},{10,9},{11,1... | collective-permute-start | bytes 884744 | tf_op jit(solution)/shard_map/ppermute | solution.py:369
  129.8 10.8 %collective-permute-start = (bf16[4,48,768]{2,1,0:T(8,128)(2,1)S(1)}, bf16[4,48,768]{2,1,0:T(8,128)(2,1)S(1)}, u32[]{:S(2)}, u32[]{:S(2)}) collective-permute-start(bf16[4,48,768]{2,1,0:T(8,128)(2,1)S(1)} %all-to-all-done.3.own_ref), channel_id=1, source_target_pairs={{0,1},{1,2},{2,3},{3,4},{4,5},{5,6},{6,7},{7,8},{8,9},{9,10},{10,1... | collective-permute-start | bytes 884744 | tf_op jit(solution)/shard_map/ppermute | solution.py:368
  140.6 11.2 %copy-start = (bf16[16,256,128]{2,1,0:T(8,128)(2,1)S(1)}, bf16[16,256,128]{2,1,0:T(8,128)(2,1)}, u32[]{:S(2)}) copy-start(bf16[16,256,128]{2,1,0:T(8,128)(2,1)} %shard_map.71.w0_ref) | copy-start | bytes 3145732
Sparse Core Ops, SparseCore 0:
  9.4 98.8 all-gather.2

commit v5 on v4

--- a/solution.py
+++ b/solution.py
@@ -257,16 +257,29 @@
             out_ref[0, rows, pair * LANES : (pair + 1) * LANES] = both.astype(BF16)
 
 
-def output_kernel(place_ref, attended_ref, hidden_ref, w0_ref, w1_ref, w2_ref, w3_ref, out_ref):
+def times_rows(group, rows, t):
+    pair = jnp.concatenate([rows[t], rows[t + 1]], axis=1)
+    return jnp.dot(group, pair, preferred_element_type=F32)
+
+
+def partial_kernel(place_ref, attended_ref, hidden_ref, w0_ref, w1_ref, out_ref):
     rep = place_ref[0]
-    weights = (w0_ref, w1_ref, w2_ref, w3_ref)
-    groups = [attended_ref[rep ^ k] for k in range(4)]
+    groups = [attended_ref[rep ^ k] for k in (0, 1)]
+    for t in range(0, CHUNKS, 2):
+        lanes = slice(t * LANES, (t + 2) * LANES)
+        total = hidden_ref[:, lanes].astype(F32)
+        for group, rows in zip(groups, (w0_ref, w1_ref)):
+            total = total + times_rows(group, rows, t)
+        out_ref[:, lanes] = total
+
+
+def output_kernel(place_ref, attended_ref, total_ref, w2_ref, w3_ref, out_ref):
+    group_2 = attended_ref[place_ref[0] ^ 2]
+    group_3 = attended_ref[place_ref[0] ^ 3]
     chunks = []
     for t in range(0, CHUNKS, 2):
-        total = hidden_ref[:, t * LANES : (t + 2) * LANES].astype(F32)
-        for k in range(4):
-            pair = jnp.concatenate([weights[k][t], weights[k][t + 1]], axis=1)
-            total = total + jnp.dot(groups[k], pair, preferred_element_type=F32)
+        total = total_ref[:, t * LANES : (t + 2) * LANES] + times_rows(group_2, w2_ref, t)
+        total = total + times_rows(group_3, w3_ref, t)
         chunks.append(total[:, 0:LANES])
         chunks.append(total[:, LANES : 2 * LANES])
     lane = lax.broadcasted_iota(jnp.int32, (256, LANES), 1)
@@ -398,15 +411,25 @@
         out_specs=pl.BlockSpec((1, 256, 256), lambda p: (p, 0, 0)),
     )(project_left, project, project_right, keys, query, key_scale, query_scale, bias)
 
+    group = rep.astype(jnp.int32).reshape(1)
+    total = call(
+        partial_kernel,
+        jax.ShapeDtypeStruct((256, WIDE), F32),
+        32,
+        1000,
+        6000,
+        in_specs=[smem] + [vmem] * 4,
+        out_specs=vmem,
+    )(group, attended, hidden, own_rows, near_rows)
     result = call(
         output_kernel,
         jax.ShapeDtypeStruct((256, WIDTH), BF16),
         32,
-        1000,
-        6000,
-        in_specs=[smem] + [vmem] * 6,
+        300,
+        3000,
+        in_specs=[smem] + [vmem] * 4,
         out_specs=vmem,
-    )(rep.astype(jnp.int32).reshape(1), attended, hidden, own_rows, near_rows, far_rows, last_rows)
+    )(group, attended, total, far_rows, last_rows)
     return result.reshape(4, 8, 8, WIDTH)
 
 

time: 162 us -> 161 us (level)
  waiting for transfers between devices: 18.7 us -> 16.3 us
    ppermute x1, waiting for transfers between devices: 3.35 us -> 1.56 us  [body(): far_rows = lax.ppermute(own_rows, 'rep', [(i, i ^ 2) for i in range(4)])]
  transfers between devices with their start and end apart: 10 -> 10, of which waited for: 5 -> 5; matrix products, arithmetic and copies ran while one was open for 0% -> 0% of each run, Pallas kernels for 13% -> 14%
where the time goes in v5:
time: 161 us; the launch traced here: 160 us
  blocking collectives  71.5 us (44%)
  starting transfers between devices  32.5 us (20%)
  Pallas kernels  26.4 us (16%)
  waiting for transfers between devices  16.3 us (10%)
  between operations  13.6 us (8%)
    all_to_all x1, blocking collectives, body(): lax.all_to_all(message, 'tx', split_axis=0, concat_axis=0, tiled=True)  47 us
    all_to_all x1, blocking collectives, body(): cells = lax.all_to_all(cells, 'ty', split_axis=0, concat_axis=0, tiled=True)  16 us
    all_to_all x1, waiting for transfers between devices, body(): lax.all_to_all(sums.reshape(32, CELLS, 256), ('rep', 'ty'), split_axis=0,...  12.2 us
    pallas_call x1, Pallas kernels, body(): call(attend_kernel, jax.ShapeDtypeStruct((4, 256, 256), BF16), 48, 8000,...  8.83 us
    all_gather x1, blocking collectives, body(): gained = lax.all_gather(gained, 'rep', axis=0, tiled=True)  8.38 us
    all_to_all x1, starting transfers between devices, body(): lax.all_to_all(sums.reshape(32, CELLS, 256), ('rep', 'ty'), split_axis=0,...  6 us
    ppermute x1, starting transfers between devices, body(): lax.ppermute(own_rows, ('rep', 'ty'), [(r * 8 + y, (r ^ 3) * 8 + (y ^ 4))...  5.76 us
    ppermute x1, starting transfers between devices, body(): project_left = lax.ppermute(project, 'tx', to_right)  5.26 us
  transfers between devices with their start and end apart: 10, of which 5 were waited for; matrix products, arithmetic and copies ran while one was open for 0% of the time, Pallas kernels for 14%

profile of v5, /device:TPU:24, one launch (start us, length us, event | category | flops | bytes accessed | tf_op | source)
XLA Modules:
  0.0 160.4 jit_solution(8514182595070148941)
XLA Ops:
  6.5 2.1 %shard_map.64 = (bf16[16,120,128]{2,1,0:T(8,128)(2,1)}, bf16[176,768]{1,0:T(8,128)(2,1)}) custom-call(s32[1]{0:T(128)} %bitcast.1.place_ref, bf16[1,2,32,768]{3,2,1,0:T(8,128)(2,1)} %latent_hbm.1, bf16[48,1920]{1,0:T(8,128)(2,1)} %weight_hbm.1, bf16[120,768]{1,0:T(8,128)(2,1)} %qkv_hbm.1, bf16[120,256]{1,0:T(8,128)(2,1)} %bitcast.16), custom_call_target="tpu_custom_call" | custom-call | flops 10000000 | bytes 500000 | tf_op jit(solution)/shard_map/pallas_call | solution.py:302
  8.7 47.0 %all_to_all.20.moved_ref = bf16[16,120,128]{2,1,0:T(8,128)(2,1)S(1)} all-to-all(bf16[16,120,128]{2,1,0:T(8,128)(2,1)} %get-tuple-element.15), channel_id=1, replica_groups=mesh['rep'=4,'ty'=8,'tx'=16] {'tx'}, dimensions={0} | all-to-all | bytes 983040 | tf_op jit(solution)/shard_map/all_to_all | solution.py:319
  55.8 16.0 %all_to_all.21 = bf16[8,64,768]{2,1,0:T(8,128)(2,1)S(1)} all-to-all(bf16[8,64,768]{2,1,0:T(8,128)(2,1)S(1)} %shard_map.65), channel_id=1, replica_groups=mesh['rep'=4,'ty'=8,'tx'=16] {'ty'}, dimensions={0} | all-to-all | bytes 1572864 | tf_op jit(solution)/shard_map/all_to_all | solution.py:321
  71.8 1.3 shard_map.66
  73.1 6.0 %all-to-all-start.2 = ((bf16[32,48,256]{2,1,0:T(8,128)(2,1)}), bf16[32,48,256]{2,1,0:T(8,128)(2,1)S(1)}, u32[]{:S(2)}, u32[]{:S(2)}) async-start(bf16[32,48,256]{2,1,0:T(8,128)(2,1)} %bitcast.4), calls=%async_computation.2 | async-start | bytes 1572864 | tf_op jit(solution)/shard_map/all_to_all | solution.py:325
  79.2 12.2 %all-to-all-done.2.parts_ref = bf16[32,48,256]{2,1,0:T(8,128)(2,1)S(1)} async-done(((bf16[32,48,256]{2,1,0:T(8,128)(2,1)}), bf16[32,48,256]{2,1,0:T(8,128)(2,1)S(1)}, u32[]{:S(2)}, u32[]{:S(2)}) %all-to-all-start.2) | async-done | bytes 786464 | tf_op jit(solution)/shard_map/all_to_all | solution.py:325
  91.4 0.8 shard_map.67
  92.2 1.3 collective-permute-start.3
  93.5 5.2 %collective-permute-start.2 = (bf16[48,2048]{1,0:T(8,128)(2,1)}, bf16[48,2048]{1,0:T(8,128)(2,1)}, u32[]{:S(2)}, u32[]{:S(2)}) collective-permute-start(bf16[48,2048]{1,0:T(8,128)(2,1)} %get-tuple-element.18.own_ref), channel_id=1, source_target_pairs={{0,1},{1,2},{2,3},{3,4},{4,5},{5,6},{6,7},{7,8},{8,9},{9,10},{10,1... | collective-permute-start | bytes 589832 | tf_op jit(solution)/shard_map/ppermute | solution.py:336
  98.8 8.4 %all_gather.9.gained_ref = bf16[192,2048]{1,0:T(8,128)(2,1)} all-gather(bf16[48,2048]{1,0:T(8,128)(2,1)S(1)} %get-tuple-element.16), channel_id=1, replica_groups=mesh['rep'=4,'ty'=8,'tx'=16] {'rep'}, dimensions={0}, use_global_device_ids=true | all-gather | bytes 983040 | tf_op jit(solution)/shard_map/all_gather | solution.py:338
  107.2 1.2 all-gather.3.cloned.1.call-done
  108.4 4.3 %shard_map.68.after_ref = bf16[192,768]{1,0:T(8,128)(2,1)} custom-call(bf16[192,2048]{1,0:T(8,128)(2,1)} %all_gather.9.gained_ref, bf16[16,176,768]{2,1,0:T(8,128)(2,1)} %bitcast.13), custom_call_target="tpu_custom_call" | custom-call | flops 1000000000 | bytes 6000000 | tf_op jit(solution)/shard_map/pallas_call | solution.py:358
  112.7 3.5 %all-to-all-start.3 = ((bf16[4,48,768]{2,1,0:T(8,128)(2,1)}), bf16[4,48,768]{2,1,0:T(8,128)(2,1)S(1)}, u32[]{:S(2)}, u32[]{:S(2)}) async-start(bf16[4,48,768]{2,1,0:T(8,128)(2,1)} %bitcast.15), calls=%async_computation.3 | async-start | bytes 589824 | tf_op jit(solution)/shard_map/all_to_all | solution.py:378
  116.2 2.3 %shard_map.71.w0_ref = bf16[16,256,128]{2,1,0:T(8,128)(2,1)} custom-call(bf16[16,176,768]{2,1,0:T(8,128)(2,1)} %bitcast.14, bf16[192,768]{1,0:T(8,128)(2,1)} %shard_map.68.after_ref), custom_call_target="tpu_custom_call" | custom-call | flops 3000000000 | bytes 3000000 | tf_op jit(solution)/shard_map/pallas_call | solution.py:368
  118.5 5.8 %collective-permute-start.6 = (bf16[16,256,128]{2,1,0:T(8,128)(2,1)}, bf16[16,256,128]{2,1,0:T(8,128)(2,1)S(1)}, u32[]{:S(2)}, u32[]{:S(2)}) collective-permute-start(bf16[16,256,128]{2,1,0:T(8,128)(2,1)} %shard_map.71.w0_ref), channel_id=1, source_target_pairs={{0,448},{16,464},{32,480},{48,496},{64,384},{80,400},{96,416},{112... | collective-permute-start | bytes 3145736 | tf_op jit(solution)/shard_map/ppermute | solution.py:386
  124.3 1.9 %collective-permute-start.5 = (bf16[16,256,128]{2,1,0:T(8,128)(2,1)}, bf16[16,256,128]{2,1,0:T(8,128)(2,1)S(1)}, u32[]{:S(2)}, u32[]{:S(2)}) collective-permute-start(bf16[16,256,128]{2,1,0:T(8,128)(2,1)} %shard_map.71.w0_ref), channel_id=1, source_target_pairs={{0,256},{128,384},{256,0},{384,128},{1,257},{129,385},{257,1},{385... | collective-permute-start | bytes 3145736 | tf_op jit(solution)/shard_map/ppermute | solution.py:385
  126.2 2.3 %collective-permute-start.4 = (bf16[16,256,128]{2,1,0:T(8,128)(2,1)}, bf16[16,256,128]{2,1,0:T(8,128)(2,1)S(1)}, u32[]{:S(2)}, u32[]{:S(2)}) collective-permute-start(bf16[16,256,128]{2,1,0:T(8,128)(2,1)} %shard_map.71.w0_ref), channel_id=1, source_target_pairs={{0,128},{128,0},{256,384},{384,256},{1,129},{129,1},{257,385},{385... | collective-permute-start | bytes 3145736 | tf_op jit(solution)/shard_map/ppermute | solution.py:384
  128.5 1.3 collective-permute-start.1
  129.8 5.3 %collective-permute-start = (bf16[4,48,768]{2,1,0:T(8,128)(2,1)S(1)}, bf16[4,48,768]{2,1,0:T(8,128)(2,1)}, u32[]{:S(2)}, u32[]{:S(2)}) collective-permute-start(bf16[4,48,768]{2,1,0:T(8,128)(2,1)S(1)} %all-to-all-done.3.own_ref), channel_id=1, source_target_pairs={{0,1},{1,2},{2,3},{3,4},{4,5},{5,6},{6,7},{7,8},{8,9},{9,10},{10,1... | collective-permute-start | bytes 884744 | tf_op jit(solution)/shard_map/ppermute | solution.py:381
  135.1 4.2 %shard_map.69 = (bf16[1024,144]{1,0:T(8,128)(2,1)S(1)}, bf16[256,144]{1,0:T(8,128)(2,1)S(1)}, f32[1024,128]{1,0:T(8,128)S(1)}, f32[256,128]{1,0:T(8,128)S(1)}, f...) custom-call(s32[6]{0:T(128)S(1)} %pad_add_fusion.place_ref, bf16[48,2048]{1,0:T(8,128)(2,1)} %collective-permute-done.2.left_ref, ...), custom_call_target="tpu_custom_call" | custom-call | flops 2000000000 | bytes 8000000 | tf_op jit(solution)/shard_map/pallas_call | solution.py:340
  139.5 1.1 collective-permute-done.left_ref
  140.6 8.8 %shard_map.70.attended_ref = bf16[4,256,256]{2,1,0:T(8,128)(2,1)S(1)} custom-call(bf16[4,48,768]{2,1,0:T(8,128)(2,1)} %collective-permute-done.left_ref, bf16[4,48,768]{2,1,0:T(8,128)(2,1)S(1)} %all-to-all-done.3.own_ref, bf16[4,48,768]{2,1,0:T(8,128)(2,1)} %collective-permute-done.1.right_ref, bf16[1024,144]{1,0:T(8,128)(2,1)S(1)} %get-tuple-element.19.keys_ref, ...), custom_call_target="tpu_custom_call" | custom-call | flops 8000000000 | bytes 1000000 | tf_op jit(solution)/shard_map/pallas_call | solution.py:394
  150.2 1.6 collective-permute-done.5.w2_ref
  151.8 1.7 %shard_map.73 = bf16[256,1920]{1,0:T(8,128)(2,1)} custom-call(s32[1]{0:T(128)} %bitcast.place_ref, bf16[4,256,256]{2,1,0:T(8,128)(2,1)S(1)} %shard_map.70.attended_ref, f32[256,2048]{1,0:T(8,128)S(1)} %shard_map.72.total_ref, bf16[16,256,128]{2,1,0:T(8,128)(2,1)S(1)} %collective-permute-done.5.w2_ref, bf16[16,256,128]{2,1,0:T(8,128)(2,1)S(1)} %collective-permute-done.6.w3_ref), custom_call_target="tpu_custom_call" | custom-call | flops 300000000 | bytes 3000000 | tf_op jit(solution)/shard_map/pallas_call | solution.py:424
  (19 shorter events, 1.2 us)
Async XLA Ops:
  6.5 101.8 %all-gather.3.cloned.1.call-start = ((), (), s32[]{:S(2)}) async-start(), calls=%async_computation.4 | async-start | bytes 4595712 | tf_op jit(solution)/shard_map/all_gather | solution.py:318
  8.7 70.4 %copy-start.1 = (bf16[1920]{0:T(1024)(128)(2,1)S(1)}, bf16[1920]{0:T(1024)(128)(2,1)}, u32[]{:S(2)}) copy-start(bf16[1920]{0:T(1024)(128)(2,1)} %param.10) | copy-start | bytes 11524
  73.1 18.4 %all-to-all-start.2 = ((bf16[32,48,256]{2,1,0:T(8,128)(2,1)}), bf16[32,48,256]{2,1,0:T(8,128)(2,1)S(1)}, u32[]{:S(2)}, u32[]{:S(2)}) async-start(bf16[32,48,256]{2,1,0:T(8,128)(2,1)} %bitcast.4), calls=%async_computation.2 | async-start | bytes 1572864 | tf_op jit(solution)/shard_map/all_to_all | solution.py:325
  92.2 36.2 %collective-permute-start.3 = (bf16[48,2048]{1,0:T(8,128)(2,1)}, bf16[48,2048]{1,0:T(8,128)(2,1)}, u32[]{:S(2)}, u32[]{:S(2)}) collective-permute-start(bf16[48,2048]{1,0:T(8,128)(2,1)} %get-tuple-element.18.own_ref), channel_id=1, source_target_pairs={{1,0},{2,1},{3,2},{4,3},{5,4},{6,5},{7,6},{8,7},{9,8},{10,9},{11,1... | collective-permute-start | bytes 589832 | tf_op jit(solution)/shard_map/ppermute | solution.py:337
  93.5 36.3 %collective-permute-start.2 = (bf16[48,2048]{1,0:T(8,128)(2,1)}, bf16[48,2048]{1,0:T(8,128)(2,1)}, u32[]{:S(2)}, u32[]{:S(2)}) collective-permute-start(bf16[48,2048]{1,0:T(8,128)(2,1)} %get-tuple-element.18.own_ref), channel_id=1, source_target_pairs={{0,1},{1,2},{2,3},{3,4},{4,5},{5,6},{6,7},{7,8},{8,9},{9,10},{10,1... | collective-permute-start | bytes 589832 | tf_op jit(solution)/shard_map/ppermute | solution.py:336
  112.7 15.8 %all-to-all-start.3 = ((bf16[4,48,768]{2,1,0:T(8,128)(2,1)}), bf16[4,48,768]{2,1,0:T(8,128)(2,1)S(1)}, u32[]{:S(2)}, u32[]{:S(2)}) async-start(bf16[4,48,768]{2,1,0:T(8,128)(2,1)} %bitcast.15), calls=%async_computation.3 | async-start | bytes 589824 | tf_op jit(solution)/shard_map/all_to_all | solution.py:378
  116.2 18.9 %copy-start.2 = (s32[1,1,4]{2,1,0:T(1,128)S(1)}, s32[1,1,4]{2,1,0:T(1,128)}, u32[]{:S(2)}) copy-start(s32[1,1,4]{2,1,0:T(1,128)} %param.11) | copy-start | bytes 52
  118.5 31.7 %collective-permute-start.6 = (bf16[16,256,128]{2,1,0:T(8,128)(2,1)}, bf16[16,256,128]{2,1,0:T(8,128)(2,1)S(1)}, u32[]{:S(2)}, u32[]{:S(2)}) collective-permute-start(bf16[16,256,128]{2,1,0:T(8,128)(2,1)} %shard_map.71.w0_ref), channel_id=1, source_target_pairs={{0,448},{16,464},{32,480},{48,496},{64,384},{80,400},{96,416},{112... | collective-permute-start | bytes 3145736 | tf_op jit(solution)/shard_map/ppermute | solution.py:386
  124.3 27.5 %collective-permute-start.5 = (bf16[16,256,128]{2,1,0:T(8,128)(2,1)}, bf16[16,256,128]{2,1,0:T(8,128)(2,1)S(1)}, u32[]{:S(2)}, u32[]{:S(2)}) collective-permute-start(bf16[16,256,128]{2,1,0:T(8,128)(2,1)} %shard_map.71.w0_ref), channel_id=1, source_target_pairs={{0,256},{128,384},{256,0},{384,128},{1,257},{129,385},{257,1},{385... | collective-permute-start | bytes 3145736 | tf_op jit(solution)/shard_map/ppermute | solution.py:385
  126.2 23.3 %collective-permute-start.4 = (bf16[16,256,128]{2,1,0:T(8,128)(2,1)}, bf16[16,256,128]{2,1,0:T(8,128)(2,1)S(1)}, u32[]{:S(2)}, u32[]{:S(2)}) collective-permute-start(bf16[16,256,128]{2,1,0:T(8,128)(2,1)} %shard_map.71.w0_ref), channel_id=1, source_target_pairs={{0,128},{128,0},{256,384},{384,256},{1,129},{129,1},{257,385},{385... | collective-permute-start | bytes 3145736 | tf_op jit(solution)/shard_map/ppermute | solution.py:384
  128.5 11.1 %collective-permute-start.1 = (bf16[4,48,768]{2,1,0:T(8,128)(2,1)S(1)}, bf16[4,48,768]{2,1,0:T(8,128)(2,1)}, u32[]{:S(2)}, u32[]{:S(2)}) collective-permute-start(bf16[4,48,768]{2,1,0:T(8,128)(2,1)S(1)} %all-to-all-done.3.own_ref), channel_id=1, source_target_pairs={{1,0},{2,1},{3,2},{4,3},{5,4},{6,5},{7,6},{8,7},{9,8},{10,9},{11,1... | collective-permute-start | bytes 884744 | tf_op jit(solution)/shard_map/ppermute | solution.py:382
  129.8 10.8 %collective-permute-start = (bf16[4,48,768]{2,1,0:T(8,128)(2,1)S(1)}, bf16[4,48,768]{2,1,0:T(8,128)(2,1)}, u32[]{:S(2)}, u32[]{:S(2)}) collective-permute-start(bf16[4,48,768]{2,1,0:T(8,128)(2,1)S(1)} %all-to-all-done.3.own_ref), channel_id=1, source_target_pairs={{0,1},{1,2},{2,3},{3,4},{4,5},{5,6},{6,7},{7,8},{8,9},{9,10},{10,1... | collective-permute-start | bytes 884744 | tf_op jit(solution)/shard_map/ppermute | solution.py:381
  140.6 8.8 %copy-start = (bf16[16,256,128]{2,1,0:T(8,128)(2,1)S(1)}, bf16[16,256,128]{2,1,0:T(8,128)(2,1)}, u32[]{:S(2)}) copy-start(bf16[16,256,128]{2,1,0:T(8,128)(2,1)} %shard_map.71.w0_ref) | copy-start | bytes 3145732
Sparse Core Ops, SparseCore 0:
  9.4 98.8 all-gather.2
